TPU v7x, 128 devices: a whole 4x4x4 slice. The times are simulated.
128 devices in a mesh: row: 32 (over z, x_lo, y), col: 4 (over x_hi, core).
Axes of the slice: x: 4 (x_hi: 2, x_lo: 2; x = x_hi * 2 + x_lo), y: 4, z: 4, core: 2. Of those that a mesh axis runs over, the one named last changes fastest.
Arguments:
- text_hidden: bfloat16 [768, 256, 1024], P(('row', 'col')), may hold values from -8 to 8
- lengths: int32 [768], P(('row', 'col')), may hold values from 32 to 256, as said below
- up_weight: bfloat16 [4096, 1024], P(('row', 'col')), may hold values from -0.1875 to 0.1875
- up_bias: bfloat16 [4096], P(('row', 'col')), may hold values from -2 to 2
- down_weight: bfloat16 [4096, 1024], P(('row', 'col')), may hold values from -0.125 to 0.125
- ln_gain: float32 [1024], replicated, may hold values from 0.1 to 1.9
- proj_weight: bfloat16 [1024, 256], replicated, may hold values from -0.1875 to 0.1875
- graph_emb: float32 [768, 256], P('row'), may hold values from -6 to 6
- perm: int32 [768], replicated, may hold values from 0 to 767, each once
Outputs:
- loss: float32 [], replicated
- grad_graph: float32 [768, 256], P('row')
- grad_text: float32 [768, 256], P(('row', 'col'))
- grad_proj: float32 [1024, 256], P(('row', 'col'))
Inputs may be any that keep to these rules, and one draw needn't show every extreme that they name: `lengths`: number of valid tokens of each description; the first description is full.
All inputs are finite; a program needn't handle non-finite values.
Results may differ from a plain program's by a relative error of at most 0.0056.
Values may be sent and summed in bfloat16 or wider, within the bound.
No kernel may reach another device: no remote copies, remote signals or barrier semaphores. Data moves between devices by JAX's collectives and lax.ppermute only.
A program may use at most 128 MiB of HBM per device.

v0:
```python
import jax
import jax.numpy as jnp
from jax import lax
from jax.sharding import PartitionSpec as P

sharpness_divisor = 0.02
epsilon = 1e-06


def hidden_block(tokens_in, weight_in, bias_in, weight_out):
    preact = lax.dot_general(
        tokens_in, weight_in, (((1,), (1,)), ((), ())), preferred_element_type=jnp.float32
    ) + bias_in.astype(jnp.float32)
    active = jax.nn.gelu(preact, approximate=False).astype(jnp.bfloat16)
    return jnp.dot(active, weight_out, preferred_element_type=jnp.float32)


def norm_pool(tokens_in, ffn_out, ln_gain, lengths, seq_count, seq_len):
    summed = tokens_in.astype(jnp.float32) + ffn_out
    centre = summed - jnp.mean(summed, axis=-1, keepdims=True)
    spread = jnp.mean(centre * centre, axis=-1, keepdims=True)
    normed = centre * lax.rsqrt(spread + epsilon) * ln_gain
    normed = normed.reshape(seq_count, seq_len, -1)
    valid = (jnp.arange(seq_len, dtype=jnp.int32)[None, :] < lengths[:, None]).astype(jnp.float32)
    return jnp.sum(normed * valid[:, :, None], axis=1) / lengths[:, None].astype(jnp.float32)


def unit_rows(values):
    norm_rows = jnp.sqrt(jnp.sum(values * values, axis=-1, keepdims=True) + epsilon)
    return (values / norm_rows, norm_rows)


def shards(
    text_hidden, lengths, up_weight, up_bias, down_weight, ln_gain, proj_weight, graph_emb, perm
):
    seq_count, seq_len, width = text_hidden.shape
    flat_tokens = text_hidden.reshape(seq_count * seq_len, width)
    ffn_out = hidden_block(
        flat_tokens,
        lax.all_gather(up_weight, ("row", "col"), axis=0, tiled=True),
        lax.all_gather(up_bias, ("row", "col"), axis=0, tiled=True),
        lax.all_gather(down_weight, ("row", "col"), axis=0, tiled=True),
    )
    pooled = norm_pool(flat_tokens, ffn_out, ln_gain, lengths, seq_count, seq_len).astype(
        jnp.bfloat16
    )
    text_emb = jnp.dot(pooled, proj_weight, preferred_element_type=jnp.float32)
    text_unit, text_norm = unit_rows(text_emb)
    graph_unit, graph_norm = unit_rows(graph_emb)
    text_send = text_unit.astype(jnp.bfloat16)
    molecule_dispatched = graph_unit.astype(jnp.bfloat16)
    text_all = lax.all_gather(text_send, ("row", "col"), axis=0, tiled=True)
    total_pairs = perm.shape[0]
    row_count = lax.axis_size("row")
    col_count = lax.axis_size("col")
    row_index = lax.axis_index("row")
    col_index = lax.axis_index("col")
    row_block = graph_emb.shape[0]
    panel = total_pairs // col_count
    row_first = row_index * row_block
    col_first = col_index * panel
    row_ids = row_first + jnp.arange(row_block, dtype=jnp.int32)
    col_ids = col_first + jnp.arange(panel, dtype=jnp.int32)
    col_pick = (perm[:, None] == col_ids[None, :]).astype(jnp.bfloat16)
    row_pick = (perm[:, None] == row_ids[None, :]).astype(jnp.bfloat16)
    contract_first = (((0,), (0,)), ((), ()))
    text_panel = lax.dot_general(
        col_pick, text_all, contract_first, preferred_element_type=jnp.float32
    ).astype(jnp.bfloat16)
    text_diag = lax.dot_general(
        row_pick, text_all, contract_first, preferred_element_type=jnp.float32
    ).astype(jnp.bfloat16)
    pairwise_scores = (
        lax.dot_general(
            molecule_dispatched,
            text_panel,
            (((1,), (1,)), ((), ())),
            preferred_element_type=jnp.float32,
        )
        / sharpness_divisor
    )
    diag_logit = (
        jnp.sum(molecule_dispatched.astype(jnp.float32) * text_diag.astype(jnp.float32), axis=-1)
        / sharpness_divisor
    )
    expo = jnp.exp(pairwise_scores)
    row_part = jnp.sum(expo, axis=1)
    col_part = jnp.sum(expo, axis=0)
    row_total = lax.psum(row_part, "col")
    col_total = lax.psum(col_part, "row")
    row_term = jnp.sum(jnp.log(row_total)) - 2.0 * jnp.sum(diag_logit)
    col_term = jnp.sum(jnp.log(col_total))
    local_loss = jnp.where(col_index == 0, row_term, 0.0) + jnp.where(row_index == 0, col_term, 0.0)
    loss = lax.psum(local_loss, ("row", "col")) / (2.0 * total_pairs)
    matched = (row_ids[:, None] == col_ids[None, :]).astype(jnp.float32)
    sublevel_parameters = (
        (expo / row_total[:, None] + expo / col_total[None, :]) * 0.5 - matched
    ).astype(jnp.bfloat16)
    molecule_share = jnp.dot(sublevel_parameters, text_panel, preferred_element_type=jnp.float32)
    text_part = lax.dot_general(
        sublevel_parameters, molecule_dispatched, contract_first, preferred_element_type=jnp.float32
    )
    molecule_derivative_unitized = lax.psum(molecule_share, "col") / sharpness_divisor
    grad_graph = (
        molecule_derivative_unitized
        - graph_unit * jnp.sum(graph_unit * molecule_derivative_unitized, axis=-1, keepdims=True)
    ) / graph_norm
    own_first = (row_index * col_count + col_index) * seq_count
    own_perm = lax.dynamic_slice(perm, (own_first,), (seq_count,))
    grid_rows = lax.psum_scatter(text_part, "row", scatter_dimension=0, tiled=True)
    every_row = lax.all_gather(grid_rows, ("row", "col"), axis=0, tiled=True)
    sub_rows = panel // row_count
    col_block = own_perm // panel
    row_slot = own_perm % panel // sub_rows
    located = (row_slot * col_count + col_block) * sub_rows + own_perm % sub_rows
    caption_derivative_aggregate = jnp.take(every_row, located, axis=0)
    caption_derivative_unitized = caption_derivative_aggregate / sharpness_divisor
    grad_text = (
        caption_derivative_unitized
        - text_unit * jnp.sum(text_unit * caption_derivative_unitized, axis=-1, keepdims=True)
    ) / text_norm
    pooled_wide = pooled.astype(jnp.float32)
    grad_proj = lax.psum_scatter(
        lax.dot_general(
            pooled_wide,
            grad_text,
            contract_first,
            precision=lax.Precision.HIGHEST,
            preferred_element_type=jnp.float32,
        ),
        ("row", "col"),
        scatter_dimension=0,
        tiled=True,
    )
    return (loss, grad_graph, grad_text, grad_proj)


def solution(mesh):
    return jax.shard_map(
        shards,
        mesh=mesh,
        in_specs=(
            P(("row", "col"), None, None),
            P(("row", "col")),
            P(("row", "col"), None),
            P(("row", "col")),
            P(("row", "col"), None),
            P(),
            P(),
            P("row", None),
            P(),
        ),
        out_specs=(P(), P("row", None), P(("row", "col"), None), P(("row", "col"), None)),
        check_vma=False,
    )
```

profile of v0, /device:TPU:0, one launch (start us, length us, event | category | flops | bytes accessed | tf_op | source)
XLA Modules:
  0.0 1626.8 jit_solution(14374306341630194539)
XLA Ops:
  9.6 68.3 %all-reduce = bf16[4096]{0:T(1024)(128)(2,1)S(1)} all-reduce(bf16[4096]{0:T(1024)(128)(2,1)S(1)} %dynamic-update-slice), channel_id=1, replica_groups=mesh['row'=32,'col'=4] {'row','col'}, use_global_device_ids=true, to_apply=%add | all-reduce | flops 4096 | bytes 16384
  77.9 1.2 convert_element_type.55
  81.6 1.3 fusion.45
  82.9 132.8 %all-gather.5.cloned.1.call-done = bf16[4096,1024]{1,0:T(8,128)(2,1)} async-done(((bf16[32,1024]{1,0:T(8,128)(2,1)}), bf16[4096,1024]{1,0:T(8,128)(2,1)}) %all-gather.5.cloned.1.call-update) | async-done | bytes 8388624 | tf_op jit(solution)/shard_map/all_gather | solution.py:40
  215.6 69.6 %fusion.3.clone.3.clone.4 = bf16[1536,4096]{1,0:T(8,128)(2,1)} fusion(bf16[1536,1024]{1,0:T(8,128)(2,1)} %bitcast.27, bf16[4096,1024]{1,0:T(8,128)(2,1)} %all-gather.5.cloned.1.call-done, f32[4096]{0:T(1024)S(1)} %convert_element_type.52), kind=kOutput, calls=%fused_computation.4.clone.clone.clone.clone.clone.clone.clone.1 | convolution fusion | flops 13300137984 | bytes 24133632 | tf_op jit(solution)/shard_map/dot_general | solution.py:11
  285.2 133.8 %all-gather.7.cloned.1.call-done = bf16[4096,1024]{1,0:T(8,128)(2,1)} async-done(((bf16[32,1024]{1,0:T(8,128)(2,1)}), bf16[4096,1024]{1,0:T(8,128)(2,1)}) %all-gather.7.cloned.1.call-update) | async-done | bytes 8388624 | tf_op jit(solution)/shard_map/all_gather | solution.py:42
  419.0 18.7 %fusion.84 = (f32[1536]{0:T(1024)S(1)}, f32[1536,1024]{1,0:T(8,128)S(1)}) fusion(bf16[4096,1024]{1,0:T(8,128)(2,1)} %all-gather.7.cloned.1.call-done, bf16[1536,1024]{1,0:T(8,128)(2,1)} %bitcast.28, bf16[1536,4096]{1,0:T(8,128)(2,1)} %fusion.3.clone.3.clone.4), kind=kOutput, calls=%fused_computation.130 | convolution fusion | flops 12889618432 | bytes 30414848 | tf_op jit(solution)/shard_map/dot_general | solution.py:15
  440.8 175.3 %all-gather = bf16[128,6,256]{2,1,0:T(8,128)(2,1)S(1)} all-gather(bf16[1,6,256]{2,1,0:T(8,128)(2,1)S(1)} %convert_bitcast_fusion), channel_id=1, replica_groups=mesh['row'=32,'col'=4] {'row','col'}, dimensions={0}, use_global_device_ids=true | all-gather | bytes 396288 | tf_op jit(solution)/shard_map/all_gather | solution.py:52
  617.1 76.8 %psum.29 = f32[192]{0:T(256)S(1)} all-reduce(f32[192]{0:T(256)S(1)} %get-tuple-element.4), channel_id=1, replica_groups=mesh['row'=32,'col'=4] {'row'}, use_global_device_ids=true, to_apply=%region_11.0 | all-reduce | flops 192 | bytes 1536 | tf_op jit(solution)/shard_map/psum | solution.py:90
  693.9 7.2 psum.28
  701.3 79.6 %fusion = f32[8,256]{1,0:T(8,128)S(1)} fusion(f32[192,256]{1,0:T(8,128)S(1)} %fusion.76), kind=kCustom, calls=%all-reduce-scatter | all-reduce-scatter fusion | flops 65537 | bytes 205312
  781.0 3.9 collective-permute-start
  784.9 1.3 collective-permute-start.1
  786.2 1.3 collective-permute-start.7
  787.6 1.3 collective-permute-start.2
  788.9 1.3 collective-permute-start.3
  790.2 1.3 collective-permute-start.4
  791.5 8.9 collective-permute-start.5
  800.5 6.5 collective-permute-start.6
  809.0 173.1 %all-gather.1 = f32[128,6,256]{2,1,0:T(8,128)S(1)} all-gather(f32[1,6,256]{2,1,0:T(8,128)S(1)} %dynamic-slice_bitcast_fusion), channel_id=1, replica_groups=mesh['row'=32,'col'=4] {'row','col'}, dimensions={0}, use_global_device_ids=true | all-gather | bytes 792576 | tf_op jit(solution)/shard_map/all_gather | solution.py:111
  983.0 1.7 fusion.80
  989.1 64.2 %psum.30 = f32[]{:T(128)} all-reduce(f32[]{:T(128)S(6)} %add.119), channel_id=1, replica_groups=mesh['row'=32,'col'=4] {'row','col'}, use_global_device_ids=true, to_apply=%region_13.14 | all-reduce | flops 1 | bytes 8 | tf_op jit(solution)/shard_map/psum | solution.py:94
  1054.1 14.6 psum.31
  1069.6 549.6 %reduce-scatter.4.cloned.1.call-done = f32[8,256]{1,0:T(8,128)} async-done(((f32[1024,256]{1,0:T(8,128)}), f32[8,256]{1,0:T(8,128)}) %reduce-scatter.4.cloned.1.call-update) | async-done | bytes 8208 | tf_op jit(solution)/shard_map/reduce_scatter | solution.py:123
  (72 shorter events, 14.9 us)
Async XLA Ops:
  7.2 433.2 %copy-start = (bf16[1024,256]{1,0:T(8,128)(2,1)S(1)}, bf16[1024,256]{1,0:T(8,128)(2,1)}, u32[]{:S(2)}) copy-start(bf16[1024,256]{1,0:T(8,128)(2,1)} %param.15) | copy-start | bytes 1572868
  7.2 208.5 %all-gather.5.cloned.1.call-start = ((), (), s32[]{:S(2)}) async-start(), calls=%async_computation.1 | async-start | bytes 8454144 | tf_op jit(solution)/shard_map/all_gather | solution.py:40
  7.9 411.1 %all-gather.7.cloned.1.call-start = ((), (), s32[]{:S(2)}) async-start(), calls=%async_computation.2 | async-start | bytes 8454144 | tf_op jit(solution)/shard_map/all_gather | solution.py:42
  8.7 1610.5 %reduce-scatter.4.cloned.1.call-start = ((), (), s32[]{:S(2)}) async-start(), calls=%async_computation.3 | async-start | bytes 1056768 | tf_op jit(solution)/shard_map/reduce_scatter | solution.py:123
  285.2 153.4 %copy-start.4 = (f32[1024]{0:T(1024)S(1)}, f32[1024]{0:T(1024)}, u32[]{:S(2)}) copy-start(f32[1024]{0:T(1024)} %param.14) | copy-start | bytes 12292
  437.7 2.0 copy-start.3
  437.8 2.6 copy-start.6
  437.8 178.5 %copy-start.8 = (s32[768]{0:T(1024)S(1)}, s32[768]{0:T(1024)}, u32[]{:S(2)}) copy-start(s32[768]{0:T(1024)} %param.17) | copy-start | bytes 9220
  437.8 178.5 %copy-start.9 = (s32[192]{0:T(256)S(1)}, s32[192]{0:T(256)}, u32[]{:S(2)}) copy-start(s32[192]{0:T(256)} %iota_add_fusion) | copy-start | bytes 2308
  437.8 179.0 %copy-start.1 = (f32[24,256]{1,0:T(8,128)S(1)}, f32[24,256]{1,0:T(8,128)}, u32[]{:S(2)}) copy-start(f32[24,256]{1,0:T(8,128)} %param.16) | copy-start | bytes 73732
  437.8 179.0 %copy-start.5 = (f32[24]{0:T(128)S(1)}, f32[24]{0:T(128)}, u32[]{:S(2)}) copy-start(f32[24]{0:T(128)} %add_sqrt_fusion.1) | copy-start | bytes 292
  437.8 263.2 %copy-start.10 = (s32[24]{0:T(128)S(1)}, s32[24]{0:T(128)}, u32[]{:S(2)}) copy-start(s32[24]{0:T(128)} %iota_add_fusion.1) | copy-start | bytes 292
  438.6 368.3 %copy-start.7 = (u32[128]{0:T(128)S(1)}, u32[128]{0:T(128)}, u32[]{:S(2)}) copy-start(u32[128]{0:T(128)} %constant.159) | copy-start | bytes 1540
  781.0 10.5 collective-permute-start
  784.9 15.6 collective-permute-start.1
  786.2 4.0 collective-permute-start.7
  787.6 20.6 %collective-permute-start.2 = (f32[8,256]{1,0:T(8,128)S(1)}, f32[8,256]{1,0:T(8,128)S(1)}, u32[]{:S(2)}, u32[]{:S(2)}) collective-permute-start(f32[8,256]{1,0:T(8,128)S(1)} %fusion), channel_id=1, source_target_pairs={{0,12},{4,16},{8,20},{12,24},{16,28},{20,32},{24,36},{28,40},{32,4... | collective-permute-start | bytes 24584
  788.9 19.3 %collective-permute-start.3 = (f32[8,256]{1,0:T(8,128)S(1)}, f32[8,256]{1,0:T(8,128)S(1)}, u32[]{:S(2)}, u32[]{:S(2)}) collective-permute-start(f32[8,256]{1,0:T(8,128)S(1)} %fusion), channel_id=1, source_target_pairs={{0,16},{4,20},{8,24},{12,28},{16,32},{20,36},{24,40},{28,44},{32,4... | collective-permute-start | bytes 24584
  790.2 18.0 %collective-permute-start.4 = (f32[8,256]{1,0:T(8,128)S(1)}, f32[8,256]{1,0:T(8,128)S(1)}, u32[]{:S(2)}, u32[]{:S(2)}) collective-permute-start(f32[8,256]{1,0:T(8,128)S(1)} %fusion), channel_id=1, source_target_pairs={{0,20},{4,24},{8,28},{12,32},{16,36},{20,40},{24,44},{28,48},{32,5... | collective-permute-start | bytes 24584
  791.5 16.7 %collective-permute-start.5 = (f32[8,256]{1,0:T(8,128)S(1)}, f32[8,256]{1,0:T(8,128)S(1)}, u32[]{:S(2)}, u32[]{:S(2)}) collective-permute-start(f32[8,256]{1,0:T(8,128)S(1)} %fusion), channel_id=1, source_target_pairs={{0,24},{4,28},{8,32},{12,36},{16,40},{20,44},{24,48},{28,52},{32,5... | collective-permute-start | bytes 24584
  800.5 7.8 collective-permute-start.6
  983.0 636.1 %copy-start.2 = (f32[6,256]{1,0:T(8,128)}, f32[6,256]{1,0:T(8,128)S(1)}, u32[]{:S(2)}) copy-start(f32[6,256]{1,0:T(8,128)S(1)} %subtract_divide_fusion.1) | copy-start | bytes 18436
Sparse Core Ops, SparseCore 0:
  9.7 205.8 all-gather.4
  217.4 201.6 all-gather.6
  984.9 634.2 reduce-scatter.3
where the time goes:
time: 1630 us
  waiting for transfers between devices  818 us (50%)
  blocking collectives  659 us (40%)
  matrix products  92.1 us (6%)
  starting transfers between devices  25.8 us (2%)
  between operations  18.6 us (1%)
    reduce_scatter x1, waiting for transfers between devices, shards(): lax.psum_scatter(lax.dot_general(pooled_wide, grad_text, contract_first,...  550 us
    all_gather x1, blocking collectives, shards(): text_all = lax.all_gather(text_send, ('row', 'col'), axis=0, tiled=True)  175 us
    all_gather x1, blocking collectives, shards(): every_row = lax.all_gather(grid_rows, ('row', 'col'), axis=0, tiled=True)  173 us
    unnamed x2, blocking collectives  148 us
    all_gather x1, waiting for transfers between devices, shards(): lax.all_gather(down_weight, ('row', 'col'), axis=0, tiled=True)  134 us
    all_gather x1, waiting for transfers between devices, shards(): lax.all_gather(up_weight, ('row', 'col'), axis=0, tiled=True)  133 us
    psum x1, blocking collectives, shards(): col_total = lax.psum(col_part, 'row')  76.8 us
    dot_general x1, matrix products, hidden_block(): lax.dot_general(tokens_in, weight_in, (((1,), (1,)), ((), ())), preferred...  69.6 us
  transfers between devices with their start and end apart: 11, of which 3 were waited for; matrix products, arithmetic and copies ran while one was open for 5% of the time, Pallas kernels for 0%

commit v1 on v0

v1 whole, which is shorter than its diff:
```python
import functools

import jax
import jax.numpy as jnp
from jax import lax
from jax.experimental import pallas as pl
from jax.experimental.pallas import tpu as pltpu
from jax.sharding import PartitionSpec as P

sharpness_divisor = 0.02
epsilon = 1e-06
axes = ("row", "col")
block_rows = 256
erf_terms = (
    -5.7109417639367166e-08,
    2.812487991832313e-06,
    -4.7398178139701486e-05,
    -5.735534068662673e-05,
    0.03636491671204567,
    0.7978729605674744,
)
nt = (((1,), (1,)), ((), ()))
tn = (((0,), (0,)), ((), ()))


def flat_index(x, y, z, core):
    return (z * 8 + (x % 2) * 4 + y) * 4 + (x // 2) * 2 + core


def pairs(dx=0, dy=0, dz=0, dc=0, by_core=False):
    found = []
    for x in range(4):
        for y in range(4):
            for z in range(4):
                for core in range(2):
                    sign = -1 if by_core and core else 1
                    target = flat_index(
                        (x + sign * dx) % 4, (y + sign * dy) % 4, (z + sign * dz) % 4, core ^ dc
                    )
                    found.append((flat_index(x, y, z, core), target))
    return found


def send(value, **hop):
    return lax.ppermute(value, axes, pairs(**hop))


def from_line(value, axis):
    return [value] + [send(value, **{axis: hop}) for hop in (1, 3, 2)]


def gelu_exact(x):
    square = jnp.minimum(x * x, 25.0)
    series = jnp.full_like(square, erf_terms[0])
    for term in erf_terms[1:]:
        series = series * square + term
    half = 0.5 * x
    return half + half * jnp.tanh(x * series)


def pack_kernel(meta, source, packed, sem):
    for s in range(6):
        start = pl.multiple_of(meta[s], 16)
        copy = pltpu.make_async_copy(source.at[s], packed.at[pl.ds(start, 256)], sem)
        copy.start()
        copy.wait()


def pack_tokens(meta, text_hidden):
    seqs, seq_len, width = text_hidden.shape
    return pl.pallas_call(
        pack_kernel,
        grid_spec=pltpu.PrefetchScalarGridSpec(
            num_scalar_prefetch=1,
            grid=(),
            in_specs=[pl.BlockSpec(memory_space=pl.ANY)],
            out_specs=pl.BlockSpec(memory_space=pl.ANY),
            scratch_shapes=[pltpu.SemaphoreType.DMA],
        ),
        out_shape=jax.ShapeDtypeStruct((seqs * seq_len, width), jnp.bfloat16),
    )(meta, text_hidden)


def ffn_tiles(x, weights):
    total = None
    lane = lax.broadcasted_iota(jnp.int32, (1, 256), 1) // 64
    for first, second in zip(weights[::2], weights[1::2]):
        up = jnp.concatenate([first[0:128, :], second[0:128, :]], axis=0)
        down = jnp.concatenate([first[128:256, :], second[128:256, :]], axis=0)
        b0 = first[256:272, 0:256].astype(jnp.float32)
        b1 = second[256:272, 0:256].astype(jnp.float32)
        bias = jnp.where(
            lane < 2,
            jnp.where(lane == 0, b0[0:1], b0[8:9]),
            jnp.where(lane == 2, b1[0:1], b1[8:9]),
        )
        preact = lax.dot_general(x, up, nt, preferred_element_type=jnp.float32) + bias
        active = gelu_exact(preact).astype(jnp.bfloat16)
        part = jnp.dot(active, down, preferred_element_type=jnp.float32)
        total = part if total is None else total + part
    return total


def ffn_kernel(count, first, last, meta, x_ref, *refs):
    weights = refs[:count]
    refs = refs[count:]
    i = pl.program_id(0)
    live = i < meta[13]
    if not first:
        acc_in, refs = refs[0], refs[1:]
    if not last:
        (out_ref,) = refs

        @pl.when(live)
        def _():
            total = ffn_tiles(x_ref[...], weights)
            out_ref[...] = total if first else acc_in[...] + total

        return
    gain_ref, pooled_ref, sums = refs

    @pl.when(i == 0)
    def _():
        sums[...] = jnp.zeros_like(sums)

    @pl.when(live)
    def _():
        x = x_ref[...]
        summed = x.astype(jnp.float32) + (acc_in[...] + ffn_tiles(x, weights))
        centre = summed - jnp.mean(summed, axis=-1, keepdims=True)
        spread = jnp.mean(centre * centre, axis=-1, keepdims=True)
        normed = centre * lax.rsqrt(spread + epsilon) * gain_ref[...]
        base = i * block_rows
        row = base + lax.broadcasted_iota(jnp.int32, (block_rows, 1), 0)
        normed = jnp.where(row < meta[12], normed, 0.0)
        column = base + lax.broadcasted_iota(jnp.int32, (8, block_rows), 1)
        seq = lax.broadcasted_iota(jnp.int32, (8, block_rows), 0)
        member = jnp.zeros((8, block_rows), jnp.float32)
        for s in range(6):
            inside = (column >= meta[s]) & (column < meta[s] + meta[6 + s]) & (seq == s)
            member = jnp.where(inside, 1.0, member)
        sums[...] += jnp.dot(
            member, normed, precision=lax.Precision.HIGHEST, preferred_element_type=jnp.float32
        )

    @pl.when(i == pl.num_programs(0) - 1)
    def _():
        seq = lax.broadcasted_iota(jnp.int32, (8, 1), 0)
        tokens = jnp.ones((8, 1), jnp.float32)
        for s in range(6):
            tokens = jnp.where(seq == s, meta[6 + s].astype(jnp.float32), tokens)
        pooled_ref[...] = (sums[...] / tokens).astype(jnp.bfloat16)


def ffn_step(meta, packed, weights, acc=None, gain=None):
    rows, width = packed.shape
    count, first, last = len(weights), acc is None, gain is not None
    steps = rows // block_rows
    row_block = pl.BlockSpec((block_rows, width), lambda i, m: (jnp.minimum(i, m[13] - 1), 0))
    whole = lambda shape: pl.BlockSpec(shape, lambda i, m: (0, 0))
    in_specs = [row_block] + [whole(w.shape) for w in weights]
    operands = [packed, *weights]
    if not first:
        in_specs.append(row_block)
        operands.append(acc)
    scratch = []
    if last:
        in_specs.append(whole((1, width)))
        operands.append(gain)
        out_shape = jax.ShapeDtypeStruct((8, width), jnp.bfloat16)
        out_specs = whole((8, width))
        scratch = [pltpu.VMEM((8, width), jnp.float32)]
    else:
        out_shape = jax.ShapeDtypeStruct((rows, width), jnp.float32)
        out_specs = row_block
    hidden = 128 * count
    return pl.pallas_call(
        functools.partial(ffn_kernel, count, first, last),
        grid_spec=pltpu.PrefetchScalarGridSpec(
            num_scalar_prefetch=1,
            grid=(steps,),
            in_specs=in_specs,
            out_specs=out_specs,
            scratch_shapes=scratch,
        ),
        out_shape=out_shape,
        compiler_params=pltpu.CompilerParams(
            dimension_semantics=("arbitrary",), vmem_limit_bytes=40 * 2**20
        ),
        cost_estimate=pl.CostEstimate(
            flops=3 * rows * hidden * width, bytes_accessed=10 * 2**20, transcendentals=0
        ),
    )(meta, *operands)


def tail_kernel(
    place,
    pooled_ref,
    proj_ref,
    graph_ref,
    own_ref,
    slot_ref,
    loss_ref,
    grad_graph_ref,
    grad_text_ref,
    grad_proj_ref,
):
    texts = pooled_ref.shape[0]
    graphs = graph_ref.shape[0]
    flat, row_first = place[0], place[1]
    pooled = pooled_ref[...]
    text_emb = jnp.dot(pooled, proj_ref[...], preferred_element_type=jnp.float32)
    text_norm = jnp.sqrt(jnp.sum(text_emb * text_emb, axis=-1, keepdims=True) + epsilon)
    text_unit = text_emb / text_norm
    text_send = text_unit.astype(jnp.bfloat16)
    graph_send = graph_ref[...]
    slot = slot_ref[...]
    valid = slot >= 0

    def scores(rows_send):
        logits = (
            lax.dot_general(rows_send, text_send, nt, preferred_element_type=jnp.float32)
            / sharpness_divisor
        )
        expo = jnp.where(valid, jnp.exp(logits), 0.0)
        return logits, expo, jnp.sum(expo, axis=1, keepdims=True)

    logits, expo, row_total = scores(graph_send)
    col_total = jnp.where(valid, jnp.sum(expo, axis=0, keepdims=True), 1.0)
    col_scale = 0.5 / col_total
    matched = lax.broadcasted_iota(jnp.int32, (graphs, texts), 0) == slot
    diagonal = jnp.sum(jnp.where(matched, logits, 0.0), axis=1, keepdims=True)
    row_terms = jnp.sum(jnp.log(row_total) - 2.0 * diagonal, axis=0, keepdims=True)
    col_terms = jnp.sum(jnp.log(col_total), axis=1, keepdims=True)
    loss_ref[...] = (row_terms + col_terms) / (2.0 * graphs)

    def weigh(expo, row_total, matched):
        weights = expo * (0.5 / row_total) + expo * col_scale
        return (weights - jnp.where(matched, 1.0, 0.0)).astype(jnp.bfloat16)

    weights = weigh(expo, row_total, matched)
    text_grad = (
        lax.dot_general(weights, graph_send, tn, preferred_element_type=jnp.float32)
        / sharpness_divisor
    )
    along = jnp.sum(text_unit * text_grad, axis=-1, keepdims=True)
    grad_text = (text_grad - text_unit * along) / text_norm
    grad_text_ref[...] = grad_text[0:8]

    own = own_ref[...]
    own_norm = jnp.sqrt(jnp.sum(own * own, axis=-1, keepdims=True) + epsilon)
    own_unit = own / own_norm
    _, own_expo, own_total = scores(own_unit.astype(jnp.bfloat16))
    own_rows = own.shape[0]
    own_matched = row_first + lax.broadcasted_iota(jnp.int32, (own_rows, texts), 0) == slot
    own_weights = weigh(own_expo, own_total, own_matched)
    graph_grad = (
        jnp.dot(own_weights, text_send, preferred_element_type=jnp.float32) / sharpness_divisor
    )
    own_along = jnp.sum(own_unit * graph_grad, axis=-1, keepdims=True)
    grad_graph_ref[...] = (graph_grad - own_unit * own_along) / own_norm

    width = pooled.shape[1]
    feature = lax.broadcasted_iota(jnp.int32, (width, 128), 0)
    wanted = flat * 8 + lax.broadcasted_iota(jnp.int32, (width, 128), 1)
    pick = (feature == wanted).astype(jnp.bfloat16)
    picked = jnp.dot(pooled, pick, preferred_element_type=jnp.float32)
    grad_proj = lax.dot_general(
        picked,
        grad_text,
        tn,
        precision=lax.Precision.HIGHEST,
        preferred_element_type=jnp.float32,
    )
    grad_proj_ref[...] = grad_proj[0:8]


def tail(place, pooled_all, proj_weight, graph_all, graph_emb, slot):
    shapes = [(1, 1), graph_emb.shape, (8, 256), (8, 256)]
    return pl.pallas_call(
        tail_kernel,
        in_specs=[pl.BlockSpec(memory_space=pltpu.SMEM)]
        + [pl.BlockSpec(memory_space=pltpu.VMEM)] * 5,
        out_specs=[pl.BlockSpec(memory_space=pltpu.VMEM)] * 4,
        out_shape=[jax.ShapeDtypeStruct(s, jnp.float32) for s in shapes],
        compiler_params=pltpu.CompilerParams(vmem_limit_bytes=48 * 2**20),
    )(place, pooled_all, proj_weight, graph_all, graph_emb, slot)


def gather_weights(up_weight, up_bias, down_weight):
    width = up_weight.shape[1]
    bias_rows = jnp.pad(up_bias.reshape(1, 32), ((0, 7), (0, width - 32)))
    own = jnp.concatenate([up_weight, down_weight, bias_rows], axis=0)
    line = from_line(own, "dz")

    def half(k):
        up = [v[16 * k : 16 * k + 16] for v in line]
        down = [v[32 + 16 * k : 48 + 16 * k] for v in line]
        bias = jnp.concatenate([v[64:65, 16 * k : 16 * k + 16] for v in line], axis=1)
        bias = jnp.pad(jnp.tile(bias, (1, width // 64)), ((0, 7), (0, 0)))
        return jnp.concatenate(up + down + [bias], axis=0)

    def join(a, b):
        return jnp.concatenate(
            [a[0:64], b[0:64], a[64:128], b[64:128], a[128:136], b[128:136]], axis=0
        )

    halves = []
    for k, (inner, outer) in enumerate((("dx", "dy"), ("dy", "dx"))):
        ring = [half(k)]
        for _ in range(3):
            ring.append(send(ring[-1], by_core=True, **{inner: 1}))
        blocks = []
        for start in (join(ring[0], ring[1]), join(ring[2], ring[3])):
            steps = [start]
            for _ in range(3):
                steps.append(send(steps[-1], by_core=True, **{outer: 1}))
            blocks.append(steps)
        halves.append(blocks)
    order = [(0, 0), (0, 1), (1, 0), (0, 2), (1, 1), (0, 3), (1, 2), (1, 3)]
    groups = []
    for at in range(0, 8, 2):
        mine, other = [], []
        for block, step in order[at : at + 2]:
            for k in range(2):
                value = halves[k][block][step]
                mine.append(value)
                other.append(send(value, dc=1))
        groups.append(mine + other)
    return groups


def shards(
    text_hidden, lengths, up_weight, up_bias, down_weight, ln_gain, proj_weight, graph_emb, perm
):
    row_index = lax.axis_index("row")
    col_index = lax.axis_index("col")
    z, y = row_index // 8, row_index % 4
    x = (col_index // 2) * 2 + (row_index // 4) % 2
    core = col_index % 2
    flat = row_index * 4 + col_index

    padded = (lengths + 15) // 16 * 16
    starts = jnp.cumsum(padded) - padded
    total = jnp.sum(padded)
    row_blocks = (total + block_rows - 1) // block_rows
    meta = jnp.concatenate(
        [starts, lengths, jnp.stack([total, row_blocks]), jnp.zeros((2,), jnp.int32)]
    ).astype(jnp.int32)

    packed = pack_tokens(meta, text_hidden)
    groups = gather_weights(up_weight, up_bias, down_weight)
    graph_norm = jnp.sqrt(jnp.sum(graph_emb * graph_emb, axis=-1, keepdims=True) + epsilon)
    graph_send = (graph_emb / graph_norm).astype(jnp.bfloat16)
    graph_all = lax.all_gather(graph_send, "row", axis=0, tiled=True)

    acc = None
    for at, group in enumerate(groups):
        gain = ln_gain.reshape(1, -1) if at == len(groups) - 1 else None
        acc = ffn_step(meta, packed, group, acc, gain)
    pooled = acc
    for axis in ("dz", "dy", "dx"):
        pooled = jnp.concatenate(from_line(pooled, axis), axis=0)
    pooled_all = jnp.concatenate([pooled, send(pooled, dc=1)], axis=0)

    rel = jnp.array([0, -1, 1, 2], jnp.int32)
    ids = flat_index(
        ((x + rel) % 4)[None, :, None, None],
        ((y + rel) % 4)[None, None, :, None],
        ((z + rel) % 4)[None, None, None, :],
        (core ^ jnp.arange(2, dtype=jnp.int32))[:, None, None, None],
    ).reshape(-1, 1)
    lane = jnp.arange(8, dtype=jnp.int32)[None, :]
    tower = jnp.where(lane < 6, ids * 6 + lane, -1).reshape(-1)
    pairs_all = perm.shape[0]
    hit = tower[None, :] == jnp.arange(pairs_all, dtype=jnp.int32)[:, None]
    slot = jnp.sum(jnp.where(hit, perm[:, None] + 1, 0), axis=0, keepdims=True) - 1
    place = jnp.stack([flat, row_index * graph_emb.shape[0]]).astype(jnp.int32)
    loss, grad_graph, grad_text, grad_proj = tail(
        place, pooled_all, proj_weight, graph_all, graph_emb, slot.astype(jnp.int32)
    )
    return (loss[0, 0], grad_graph, grad_text[:6], grad_proj)


def solution(mesh):
    return jax.shard_map(
        shards,
        mesh=mesh,
        in_specs=(
            P(("row", "col"), None, None),
            P(("row", "col")),
            P(("row", "col"), None),
            P(("row", "col")),
            P(("row", "col"), None),
            P(),
            P(),
            P("row", None),
            P(),
        ),
        out_specs=(P(), P("row", None), P(("row", "col"), None), P(("row", "col"), None)),
        check_vma=False,
    )
```

time: 1630 us -> 395 us (0.24)
  waiting for transfers between devices: 818 us -> 68.8 us
  blocking collectives: 659 us -> 82.5 us
  Pallas kernels: 0 us -> 158 us
  matrix products: 92.1 us -> 0 us
  local copies, waits for them, and re-layouts: 3.04 us -> 34 us
  starting transfers between devices: 25.8 us -> 48.2 us
  between operations: 18.6 us -> 1.97 us
    reduce_scatter x1 -> x0, waiting for transfers between devices: 550 us -> none  [shards(): lax.psum_scatter(lax.dot_general(pooled_wide, grad_text, contract_first,...]
    all_gather x2 -> x0, waiting for transfers between devices: 267 us -> none  [the longest x1 134 us: shards(): lax.all_gather(down_weight, ('row', 'col'), axis=0, tiled=True)]
    all_gather x2 -> x1, blocking collectives: 348 us -> 82.5 us  [shards(): graph_all = lax.all_gather(graph_send, 'row', axis=0, tiled=True)]
    psum x4 -> x0, blocking collectives: 163 us -> none  [the longest x1 76.8 us: shards(): col_total = lax.psum(col_part, 'row')]
    pallas_call x0 -> x6, Pallas kernels: none -> 158 us  [the longest x1 103 us: pack_tokens(): pl.pallas_call(pack_kernel, grid_spec=pltpu.PrefetchScalarGridSpec(num_sc...]
    unnamed x2 -> x0, blocking collectives: 148 us -> none
    dot_general x9 -> x0, matrix products: 92.1 us -> none  [the longest x1 69.6 us: hidden_block(): lax.dot_general(tokens_in, weight_in, (((1,), (1,)), ((), ())), preferred...]
    ppermute x0 -> x47, waiting for transfers between devices: none -> 68.8 us  [send(): return lax.ppermute(value, axes, pairs(**hop))]
  transfers between devices with their start and end apart: 11 -> 47, of which waited for: 3 -> 19; matrix products, arithmetic and copies ran while one was open for 5% -> 3% of each run, Pallas kernels for 0% -> 34%
where the time goes in v1:
time: 395 us; the launch traced here: 398 us
  Pallas kernels  158 us (40%)
  blocking collectives  82.5 us (21%)
  waiting for transfers between devices  68.8 us (17%)
  starting transfers between devices  48.2 us (12%)
  local copies, waits for them, and re-layouts  34 us (9%)
  other arithmetic  4.19 us (1%)
    pallas_call x1, Pallas kernels, pack_tokens(): pl.pallas_call(pack_kernel, grid_spec=pltpu.PrefetchScalarGridSpec(num_sc...  103 us
    all_gather x1, blocking collectives, shards(): graph_all = lax.all_gather(graph_send, 'row', axis=0, tiled=True)  82.5 us
    ppermute x47, waiting for transfers between devices, send(): return lax.ppermute(value, axes, pairs(**hop))  68.8 us
    ppermute x47, starting transfers between devices, send(): return lax.ppermute(value, axes, pairs(**hop))  48.2 us
    pallas_call x4, Pallas kernels, ffn_step(): pl.pallas_call(functools.partial(ffn_kernel, count, first, last), grid_sp...  48 us
    unnamed x101, local copies, waits for them, and re-layouts  30.5 us
  transfers between devices with their start and end apart: 47, of which 19 were waited for; matrix products, arithmetic and copies ran while one was open for 3% of the time, Pallas kernels for 34%

profile of v1, /device:TPU:0, one launch (start us, length us, event | category | flops | bytes accessed | tf_op | source)
XLA Modules:
  0.0 397.7 jit_solution(492955111535071921)
XLA Ops:
  18.5 4.5 %collective-permute-done.8 = bf16[136,1024]{1,0:T(8,128)(2,1)S(1)} collective-permute-done((bf16[136,1024]{1,0:T(8,128)(2,1)S(1)}, bf16[136,1024]{1,0:T(8,128)(2,1)S(1)}, u32[]{:S(2)}, u32[]{:S(2)}) %collective-permute-start.8) | collective-permute-done | bytes 278560 | tf_op jit(solution)/shard_map/ppermute | solution.py:45
  27.4 4.3 %collective-permute-done.3 = bf16[136,1024]{1,0:T(8,128)(2,1)S(1)} collective-permute-done((bf16[136,1024]{1,0:T(8,128)(2,1)S(1)}, bf16[136,1024]{1,0:T(8,128)(2,1)S(1)}, u32[]{:S(2)}, u32[]{:S(2)}) %collective-permute-start.3) | collective-permute-done | bytes 278560 | tf_op jit(solution)/shard_map/ppermute | solution.py:45
  32.5 2.3 collective-permute-done.9
  34.8 5.8 %collective-permute-done.4 = bf16[136,1024]{1,0:T(8,128)(2,1)S(1)} collective-permute-done((bf16[136,1024]{1,0:T(8,128)(2,1)S(1)}, bf16[136,1024]{1,0:T(8,128)(2,1)S(1)}, u32[]{:S(2)}, u32[]{:S(2)}) %collective-permute-start.4) | collective-permute-done | bytes 278560 | tf_op jit(solution)/shard_map/ppermute | solution.py:45
  40.7 5.2 %collective-permute-done.10 = bf16[136,1024]{1,0:T(8,128)(2,1)S(1)} collective-permute-done((bf16[136,1024]{1,0:T(8,128)(2,1)S(1)}, bf16[136,1024]{1,0:T(8,128)(2,1)S(1)}, u32[]{:S(2)}, u32[]{:S(2)}) %collective-permute-start.10) | collective-permute-done | bytes 278560 | tf_op jit(solution)/shard_map/ppermute | solution.py:45
  47.4 6.2 %collective-permute-done.5 = bf16[136,1024]{1,0:T(8,128)(2,1)S(1)} collective-permute-done((bf16[136,1024]{1,0:T(8,128)(2,1)S(1)}, bf16[136,1024]{1,0:T(8,128)(2,1)S(1)}, u32[]{:S(2)}, u32[]{:S(2)}) %collective-permute-start.5) | collective-permute-done | bytes 278560 | tf_op jit(solution)/shard_map/ppermute | solution.py:45
  61.4 9.1 %collective-permute-done.23.refs_3_ = bf16[272,1024]{1,0:T(8,128)(2,1)S(1)} collective-permute-done((bf16[272,1024]{1,0:T(8,128)(2,1)S(1)}, bf16[272,1024]{1,0:T(8,128)(2,1)S(1)}, u32[]{:S(2)}, u32[]{:S(2)}) %collective-permute-start.23) | collective-permute-done | bytes 557088 | tf_op jit(solution)/shard_map/ppermute | solution.py:45
  74.8 6.5 %collective-permute-done.6.refs_0_ = bf16[272,1024]{1,0:T(8,128)(2,1)} collective-permute-done((bf16[272,1024]{1,0:T(8,128)(2,1)S(1)}, bf16[272,1024]{1,0:T(8,128)(2,1)}, u32[]{:S(2)}, u32[]{:S(2)}) %collective-permute-start.6) | collective-permute-done | bytes 557088 | tf_op jit(solution)/shard_map/ppermute | solution.py:45
  84.6 4.3 %collective-permute-done.12.refs_1_ = bf16[272,1024]{1,0:T(8,128)(2,1)} collective-permute-done((bf16[272,1024]{1,0:T(8,128)(2,1)S(1)}, bf16[272,1024]{1,0:T(8,128)(2,1)}, u32[]{:S(2)}, u32[]{:S(2)}) %collective-permute-start.12) | collective-permute-done | bytes 557088 | tf_op jit(solution)/shard_map/ppermute | solution.py:45
  89.0 4.3 %collective-permute-done.7.refs_0_ = bf16[272,1024]{1,0:T(8,128)(2,1)} collective-permute-done((bf16[272,1024]{1,0:T(8,128)(2,1)}, bf16[272,1024]{1,0:T(8,128)(2,1)}, u32[]{:S(2)}, u32[]{:S(2)}) %collective-permute-start.7) | collective-permute-done | bytes 557088 | tf_op jit(solution)/shard_map/ppermute | solution.py:45
  95.2 102.7 %shard_map.129.x_ref = bf16[1536,1024]{1,0:T(8,128)(2,1)} custom-call(s32[16]{0:T(128)} %concatenate.51.meta, bf16[6,256,1024]{2,1,0:T(8,128)(2,1)} %source.1), custom_call_target="tpu_custom_call" | custom-call | tf_op jit(solution)/shard_map/pallas_call | solution.py:71
  208.3 9.7 %shard_map.130.refs_8_ = f32[1536,1024]{1,0:T(8,128)S(1)} custom-call(s32[16]{0:T(128)S(1)} %copy-done.9, bf16[1536,1024]{1,0:T(8,128)(2,1)S(1)} %copy-done, bf16[272,1024]{1,0:T(8,128)(2,1)S(1)} %copy-done.11, bf16[272,1024]{1,0:T(8,128)(2,1)S(1)} %copy-done.13, bf16[272,1024]{1,0:T(8,128)(2,1)S(1)} %copy-done.19, bf16[272,1024]{1,0:T(8,128)(2,1)S(1)} %copy-done.15, ...), custom_call_target="tpu_custom_call" | custom-call | flops 4831838208 | bytes 10485760 | tf_op jit(solution)/shard_map/pallas_call | solution.py:177
  218.0 2.6 copy-done.2
  221.7 11.2 %shard_map.131.refs_8_ = f32[1536,1024]{1,0:T(8,128)S(1)} custom-call(s32[16]{0:T(128)S(1)} %copy-done.9, bf16[1536,1024]{1,0:T(8,128)(2,1)S(1)} %copy-done, bf16[272,1024]{1,0:T(8,128)(2,1)S(1)} %constant_dynamic-update-slice_fusion.9.refs_0_, bf16[272,1024]{1,0:T(8,128)(2,1)S(1)} %constant_dynamic-update-slice_fusion.24.refs_1_, ...), custom_call_target="tpu_custom_call" | custom-call | flops 4831838208 | bytes 10485760 | tf_op jit(solution)/shard_map/pallas_call | solution.py:177
  232.9 2.6 copy-done.1
  235.5 12.1 %shard_map.132.refs_8_ = f32[1536,1024]{1,0:T(8,128)S(1)} custom-call(s32[16]{0:T(128)S(1)} %copy-done.9, bf16[1536,1024]{1,0:T(8,128)(2,1)S(1)} %copy-done, bf16[272,1024]{1,0:T(8,128)(2,1)} %collective-permute-done.6.refs_0_, bf16[272,1024]{1,0:T(8,128)(2,1)S(1)} %collective-permute-done.11.refs_1_, bf16[272,1024]{1,0:T(8,128)(2,1)} %collective-permute-done.21.refs_2_, ...), custom_call_target="tpu_custom_call" | custom-call | flops 4831838208 | bytes 10485760 | tf_op jit(solution)/shard_map/pallas_call | solution.py:177
  247.6 15.1 %shard_map.133 = bf16[8,1024]{1,0:T(8,128)(2,1)S(1)} custom-call(s32[16]{0:T(128)S(1)} %copy-done.9, bf16[1536,1024]{1,0:T(8,128)(2,1)S(1)} %copy-done, bf16[272,1024]{1,0:T(8,128)(2,1)} %collective-permute-done.7.refs_0_, bf16[272,1024]{1,0:T(8,128)(2,1)} %collective-permute-done.12.refs_1_, bf16[272,1024]{1,0:T(8,128)(2,1)} %collective-permute-done.13.refs_2_, ...), custom_call_target="tpu_custom_call" | custom-call | flops 4831838208 | bytes 10485760 | tf_op jit(solution)/shard_map/pallas_call | solution.py:177
  267.7 3.5 collective-permute-done.39
  272.0 11.2 %collective-permute-start.41 = (bf16[32,1024]{1,0:T(8,128)(2,1)S(1)}, bf16[32,1024]{1,0:T(8,128)(2,1)S(1)}, u32[]{:S(2)}, u32[]{:S(2)}) collective-permute-start(bf16[32,1024]{1,0:T(8,128)(2,1)S(1)} %pad_maximum_fusion), channel_id=1, source_target_pairs={{0,12},{1,13},{32,44},{33,45},{64,76},{65,77},{96,108},{97,109},{4... | collective-permute-start | bytes 196616 | tf_op jit(solution)/shard_map/ppermute | solution.py:45
  289.6 7.0 %collective-permute-start.43 = (bf16[128,1024]{1,0:T(8,128)(2,1)S(1)}, bf16[128,1024]{1,0:T(8,128)(2,1)S(1)}, u32[]{:S(2)}, u32[]{:S(2)}) collective-permute-start(bf16[128,1024]{1,0:T(8,128)(2,1)S(1)} %get-tuple-element.48), channel_id=1, source_target_pairs={{0,16},{1,17},{32,48},{33,49},{64,80},{65,81},{96,112},{97,113},{4... | collective-permute-start | bytes 786440 | tf_op jit(solution)/shard_map/ppermute | solution.py:45
  296.7 2.4 collective-permute-start.45
  299.3 3.3 collective-permute-done.43
  307.8 82.5 %all_gather.3.graph_ref = bf16[768,256]{1,0:T(8,128)(2,1)S(1)} all-gather(bf16[24,256]{1,0:T(8,128)(2,1)S(1)} %divide_convert_fusion), channel_id=1, replica_groups=mesh['row'=32,'col'=4] {'row'}, dimensions={0}, use_global_device_ids=true | all-gather | bytes 405504 | tf_op jit(solution)/shard_map/all_gather | solution.py:355
  390.4 7.3 %shard_map.134 = (f32[1,1]{1,0:T(1,128)}, f32[24,256]{1,0:T(8,128)}, f32[8,256]{1,0:T(8,128)}, f32[8,256]{1,0:T(8,128)}) custom-call(s32[2]{0:T(128)S(1)} %pad_add_fusion.place, bf16[1024,1024]{1,0:T(8,128)(2,1)S(1)} %constant_dynamic-update-slice_fusion.71.pooled_ref, bf16[1024,256]{1,0:T(8,128)(2,1)S(1)} %copy-done.7, ...), custom_call_target="tpu_custom_call" | custom-call | tf_op jit(solution)/shard_map/pallas_call | solution.py:280
  (219 shorter events, 70.0 us)
Async XLA Ops:
  25.5 28.2 %collective-permute-start.22 = (bf16[272,1024]{1,0:T(8,128)(2,1)S(1)}, bf16[272,1024]{1,0:T(8,128)(2,1)S(1)}, u32[]{:S(2)}, u32[]{:S(2)}) collective-permute-start(bf16[272,1024]{1,0:T(8,128)(2,1)S(1)} %constant_dynamic-update-slice_fusion.42.refs_1_), channel_id=1, source_target_pairs={{0,16},{1,19},{32,48},{33,51},{64,80},{65,83},{96,112},{97,115},{4... | collective-permute-start | bytes 1671176 | tf_op jit(solution)/shard_map/ppermute | solution.py:45
  27.0 27.0 %collective-permute-start.34 = (bf16[272,1024]{1,0:T(8,128)(2,1)S(1)}, bf16[272,1024]{1,0:T(8,128)(2,1)S(1)}, u32[]{:S(2)}, u32[]{:S(2)}) collective-permute-start(bf16[272,1024]{1,0:T(8,128)(2,1)S(1)} %constant_dynamic-update-slice_fusion.42.refs_1_), channel_id=1, source_target_pairs={{0,1},{1,0},{32,33},{33,32},{64,65},{65,64},{96,97},{97,96},{4,5},... | collective-permute-start | bytes 1671176 | tf_op jit(solution)/shard_map/ppermute | solution.py:45
  32.1 24.4 %collective-permute-start.19 = (bf16[272,1024]{1,0:T(8,128)(2,1)S(1)}, bf16[272,1024]{1,0:T(8,128)(2,1)S(1)}, u32[]{:S(2)}, u32[]{:S(2)}) collective-permute-start(bf16[272,1024]{1,0:T(8,128)(2,1)S(1)} %constant_dynamic-update-slice_fusion.30.refs_0_), channel_id=1, source_target_pairs={{0,4},{1,13},{32,36},{33,45},{64,68},{65,77},{96,100},{97,109},{4,... | collective-permute-start | bytes 1671176 | tf_op jit(solution)/shard_map/ppermute | solution.py:45
  40.6 17.0 %collective-permute-start.33 = (bf16[272,1024]{1,0:T(8,128)(2,1)S(1)}, bf16[272,1024]{1,0:T(8,128)(2,1)S(1)}, u32[]{:S(2)}, u32[]{:S(2)}) collective-permute-start(bf16[272,1024]{1,0:T(8,128)(2,1)S(1)} %constant_dynamic-update-slice_fusion.30.refs_0_), channel_id=1, source_target_pairs={{0,1},{1,0},{32,33},{33,32},{64,65},{65,64},{96,97},{97,96},{4,5},... | collective-permute-start | bytes 1671176 | tf_op jit(solution)/shard_map/ppermute | solution.py:45
  53.6 16.8 %collective-permute-start.30 = (bf16[272,1024]{1,0:T(8,128)(2,1)S(1)}, bf16[272,1024]{1,0:T(8,128)(2,1)S(1)}, u32[]{:S(2)}, u32[]{:S(2)}) collective-permute-start(bf16[272,1024]{1,0:T(8,128)(2,1)S(1)} %constant_dynamic-update-slice_fusion.24.refs_1_), channel_id=1, source_target_pairs={{0,1},{1,0},{32,33},{33,32},{64,65},{65,64},{96,97},{97,96},{4,5},... | collective-permute-start | bytes 1671176 | tf_op jit(solution)/shard_map/ppermute | solution.py:45
  53.7 16.8 %collective-permute-start.11 = (bf16[272,1024]{1,0:T(8,128)(2,1)S(1)}, bf16[272,1024]{1,0:T(8,128)(2,1)S(1)}, u32[]{:S(2)}, u32[]{:S(2)}) collective-permute-start(bf16[272,1024]{1,0:T(8,128)(2,1)S(1)} %constant_dynamic-update-slice_fusion.24.refs_1_), channel_id=1, source_target_pairs={{0,16},{1,19},{32,48},{33,51},{64,80},{65,83},{96,112},{97,115},{4... | collective-permute-start | bytes 1671176 | tf_op jit(solution)/shard_map/ppermute | solution.py:45
  56.5 13.9 %collective-permute-start.23 = (bf16[272,1024]{1,0:T(8,128)(2,1)S(1)}, bf16[272,1024]{1,0:T(8,128)(2,1)S(1)}, u32[]{:S(2)}, u32[]{:S(2)}) collective-permute-start(bf16[272,1024]{1,0:T(8,128)(2,1)S(1)} %collective-permute-done.22.refs_3_), channel_id=1, source_target_pairs={{0,16},{1,19},{32,48},{33,51},{64,80},{65,83},{96,112},{97,115},{4... | collective-permute-start | bytes 1671176 | tf_op jit(solution)/shard_map/ppermute | solution.py:45
  58.5 12.8 %collective-permute-start.35 = (bf16[272,1024]{1,0:T(8,128)(2,1)S(1)}, bf16[272,1024]{1,0:T(8,128)(2,1)S(1)}, u32[]{:S(2)}, u32[]{:S(2)}) collective-permute-start(bf16[272,1024]{1,0:T(8,128)(2,1)S(1)} %collective-permute-done.19.refs_2_), channel_id=1, source_target_pairs={{0,1},{1,0},{32,33},{33,32},{64,65},{65,64},{96,97},{97,96},{4,5},... | collective-permute-start | bytes 1671176 | tf_op jit(solution)/shard_map/ppermute | solution.py:45
  72.2 12.3 %collective-permute-start.26 = (bf16[272,1024]{1,0:T(8,128)(2,1)S(1)}, bf16[272,1024]{1,0:T(8,128)(2,1)}, u32[]{:S(2)}, u32[]{:S(2)}) collective-permute-start(bf16[272,1024]{1,0:T(8,128)(2,1)S(1)} %collective-permute-done.11.refs_1_), channel_id=1, source_target_pairs={{0,1},{1,0},{32,33},{33,32},{64,65},{65,64},{96,97},{97,96},{4,5},... | collective-permute-start | bytes 1671176 | tf_op jit(solution)/shard_map/ppermute | solution.py:45
  74.0 15.0 %collective-permute-start.12 = (bf16[272,1024]{1,0:T(8,128)(2,1)S(1)}, bf16[272,1024]{1,0:T(8,128)(2,1)}, u32[]{:S(2)}, u32[]{:S(2)}) collective-permute-start(bf16[272,1024]{1,0:T(8,128)(2,1)S(1)} %collective-permute-done.11.refs_1_), channel_id=1, source_target_pairs={{0,16},{1,19},{32,48},{33,51},{64,80},{65,83},{96,112},{97,115},{4... | collective-permute-start | bytes 1671176 | tf_op jit(solution)/shard_map/ppermute | solution.py:45
  83.0 114.9 %collective-permute-start.21 = (bf16[272,1024]{1,0:T(8,128)(2,1)S(1)}, bf16[272,1024]{1,0:T(8,128)(2,1)}, u32[]{:S(2)}, u32[]{:S(2)}) collective-permute-start(bf16[272,1024]{1,0:T(8,128)(2,1)S(1)} %collective-permute-done.20.refs_2_), channel_id=1, source_target_pairs={{0,4},{1,13},{32,36},{33,45},{64,68},{65,77},{96,100},{97,109},{4,... | collective-permute-start | bytes 1671176 | tf_op jit(solution)/shard_map/ppermute | solution.py:45
  84.5 136.1 %collective-permute-start.25 = (bf16[272,1024]{1,0:T(8,128)(2,1)}, bf16[272,1024]{1,0:T(8,128)(2,1)}, u32[]{:S(2)}, u32[]{:S(2)}) collective-permute-start(bf16[272,1024]{1,0:T(8,128)(2,1)} %collective-permute-done.6.refs_0_), channel_id=1, source_target_pairs={{0,1},{1,0},{32,33},{33,32},{64,65},{65,64},{96,97},{97,96},{4,5},... | collective-permute-start | bytes 1671176 | tf_op jit(solution)/shard_map/ppermute | solution.py:45
  88.9 131.7 %collective-permute-start.28 = (bf16[272,1024]{1,0:T(8,128)(2,1)}, bf16[272,1024]{1,0:T(8,128)(2,1)}, u32[]{:S(2)}, u32[]{:S(2)}) collective-permute-start(bf16[272,1024]{1,0:T(8,128)(2,1)} %collective-permute-done.24.refs_3_), channel_id=1, source_target_pairs={{0,1},{1,0},{32,33},{33,32},{64,65},{65,64},{96,97},{97,96},{4,5},... | collective-permute-start | bytes 1671176 | tf_op jit(solution)/shard_map/ppermute | solution.py:45
  88.9 132.2 %collective-permute-start.14 = (bf16[272,1024]{1,0:T(8,128)(2,1)}, bf16[272,1024]{1,0:T(8,128)(2,1)}, u32[]{:S(2)}, u32[]{:S(2)}) collective-permute-start(bf16[272,1024]{1,0:T(8,128)(2,1)} %collective-permute-done.12.refs_1_), channel_id=1, source_target_pairs={{0,16},{1,19},{32,48},{33,51},{64,80},{65,83},{96,112},{97,115},{4... | collective-permute-start | bytes 1671176 | tf_op jit(solution)/shard_map/ppermute | solution.py:45
  93.2 128.0 %collective-permute-start.13 = (bf16[272,1024]{1,0:T(8,128)(2,1)}, bf16[272,1024]{1,0:T(8,128)(2,1)}, u32[]{:S(2)}, u32[]{:S(2)}) collective-permute-start(bf16[272,1024]{1,0:T(8,128)(2,1)} %collective-permute-done.7.refs_0_), channel_id=1, source_target_pairs={{0,4},{1,13},{32,36},{33,45},{64,68},{65,77},{96,100},{97,109},{4,... | collective-permute-start | bytes 1671176 | tf_op jit(solution)/shard_map/ppermute | solution.py:45
  197.9 37.6 %collective-permute-start.27 = (bf16[272,1024]{1,0:T(8,128)(2,1)}, bf16[272,1024]{1,0:T(8,128)(2,1)S(1)}, u32[]{:S(2)}, u32[]{:S(2)}) collective-permute-start(bf16[272,1024]{1,0:T(8,128)(2,1)} %collective-permute-done.21.refs_2_), channel_id=1, source_target_pairs={{0,1},{1,0},{32,33},{33,32},{64,65},{65,64},{96,97},{97,96},{4,5},... | collective-permute-start | bytes 1671176 | tf_op jit(solution)/shard_map/ppermute | solution.py:45
  220.6 26.9 %collective-permute-start.16 = (bf16[272,1024]{1,0:T(8,128)(2,1)}, bf16[272,1024]{1,0:T(8,128)(2,1)S(1)}, u32[]{:S(2)}, u32[]{:S(2)}) collective-permute-start(bf16[272,1024]{1,0:T(8,128)(2,1)} %collective-permute-done.12.refs_1_), channel_id=1, source_target_pairs={{0,1},{1,0},{32,33},{33,32},{64,65},{65,64},{96,97},{97,96},{4,5},... | collective-permute-start | bytes 1671176 | tf_op jit(solution)/shard_map/ppermute | solution.py:45
  220.6 26.9 %collective-permute-start.15 = (bf16[272,1024]{1,0:T(8,128)(2,1)}, bf16[272,1024]{1,0:T(8,128)(2,1)S(1)}, u32[]{:S(2)}, u32[]{:S(2)}) collective-permute-start(bf16[272,1024]{1,0:T(8,128)(2,1)} %collective-permute-done.7.refs_0_), channel_id=1, source_target_pairs={{0,1},{1,0},{32,33},{33,32},{64,65},{65,64},{96,97},{97,96},{4,5},... | collective-permute-start | bytes 1671176 | tf_op jit(solution)/shard_map/ppermute | solution.py:45
  221.2 26.4 %collective-permute-start.18 = (bf16[272,1024]{1,0:T(8,128)(2,1)}, bf16[272,1024]{1,0:T(8,128)(2,1)}, u32[]{:S(2)}, u32[]{:S(2)}) collective-permute-start(bf16[272,1024]{1,0:T(8,128)(2,1)} %collective-permute-done.14.refs_3_), channel_id=1, source_target_pairs={{0,1},{1,0},{32,33},{33,32},{64,65},{65,64},{96,97},{97,96},{4,5},... | collective-permute-start | bytes 1671176 | tf_op jit(solution)/shard_map/ppermute | solution.py:45
  221.2 26.4 %collective-permute-start.17 = (bf16[272,1024]{1,0:T(8,128)(2,1)}, bf16[272,1024]{1,0:T(8,128)(2,1)}, u32[]{:S(2)}, u32[]{:S(2)}) collective-permute-start(bf16[272,1024]{1,0:T(8,128)(2,1)} %collective-permute-done.13.refs_2_), channel_id=1, source_target_pairs={{0,1},{1,0},{32,33},{33,32},{64,65},{65,64},{96,97},{97,96},{4,5},... | collective-permute-start | bytes 1671176 | tf_op jit(solution)/shard_map/ppermute | solution.py:45
  271.3 15.1 %collective-permute-start.40 = (bf16[32,1024]{1,0:T(8,128)(2,1)S(1)}, bf16[32,1024]{1,0:T(8,128)(2,1)S(1)}, u32[]{:S(2)}, u32[]{:S(2)}) collective-permute-start(bf16[32,1024]{1,0:T(8,128)(2,1)S(1)} %pad_maximum_fusion), channel_id=1, source_target_pairs={{0,4},{1,5},{32,36},{33,37},{64,68},{65,69},{96,100},{97,101},{4,8... | collective-permute-start | bytes 196616 | tf_op jit(solution)/shard_map/ppermute | solution.py:45
  272.0 15.0 %collective-permute-start.41 = (bf16[32,1024]{1,0:T(8,128)(2,1)S(1)}, bf16[32,1024]{1,0:T(8,128)(2,1)S(1)}, u32[]{:S(2)}, u32[]{:S(2)}) collective-permute-start(bf16[32,1024]{1,0:T(8,128)(2,1)S(1)} %pad_maximum_fusion), channel_id=1, source_target_pairs={{0,12},{1,13},{32,44},{33,45},{64,76},{65,77},{96,108},{97,109},{4... | collective-permute-start | bytes 196616 | tf_op jit(solution)/shard_map/ppermute | solution.py:45
  289.6 13.0 %collective-permute-start.43 = (bf16[128,1024]{1,0:T(8,128)(2,1)S(1)}, bf16[128,1024]{1,0:T(8,128)(2,1)S(1)}, u32[]{:S(2)}, u32[]{:S(2)}) collective-permute-start(bf16[128,1024]{1,0:T(8,128)(2,1)S(1)} %get-tuple-element.48), channel_id=1, source_target_pairs={{0,16},{1,17},{32,48},{33,49},{64,80},{65,81},{96,112},{97,113},{4... | collective-permute-start | bytes 786440 | tf_op jit(solution)/shard_map/ppermute | solution.py:45
  307.3 83.0 %collective-permute-start.46 = (bf16[512,1024]{1,0:T(8,128)(2,1)}, bf16[512,1024]{1,0:T(8,128)(2,1)S(1)}, u32[]{:S(2)}, u32[]{:S(2)}) collective-permute-start(bf16[512,1024]{1,0:T(8,128)(2,1)} %get-tuple-element.16), channel_id=1, source_target_pairs={{0,1},{1,0},{32,33},{33,32},{64,65},{65,64},{96,97},{97,96},{4,5},... | collective-permute-start | bytes 3145736 | tf_op jit(solution)/shard_map/ppermute | solution.py:45
  (53 other events, 692.4 us)

commit v2 on v1

--- a/solution.py
+++ b/solution.py
@@ -74,31 +74,60 @@
             num_scalar_prefetch=1,
             grid=(),
             in_specs=[pl.BlockSpec(memory_space=pl.ANY)],
-            out_specs=pl.BlockSpec(memory_space=pl.ANY),
+            out_specs=pl.BlockSpec(memory_space=pltpu.VMEM),
             scratch_shapes=[pltpu.SemaphoreType.DMA],
         ),
         out_shape=jax.ShapeDtypeStruct((seqs * seq_len, width), jnp.bfloat16),
+        compiler_params=pltpu.CompilerParams(vmem_limit_bytes=16 * 2**20),
     )(meta, text_hidden)
 
 
+def merge_bias(tiles, run):
+    lane = lax.broadcasted_iota(jnp.int32, (1, tiles[0].shape[1]), 1) // run % 4
+    row = tiles[0].astype(jnp.float32)[0:1]
+    for k in range(1, 4):
+        row = jnp.where(lane == k, tiles[k].astype(jnp.float32)[0:1], row)
+    return jnp.broadcast_to(row, tiles[0].shape).astype(jnp.bfloat16)
+
+
+def split_kernel(*refs):
+    parts = refs[:4]
+    for k, out in enumerate(refs[4:]):
+        for s, part in enumerate(parts):
+            out[16 * s : 16 * s + 16, :] = part[16 * k : 16 * k + 16, :]
+            out[64 + 16 * s : 80 + 16 * s, :] = part[32 + 16 * k : 48 + 16 * k, :]
+        out[128:144, :] = merge_bias([p[64 + 16 * k : 80 + 16 * k, :] for p in parts], 16)
+
+
+def join_kernel(*refs):
+    for k, out in enumerate(refs[8:]):
+        parts = refs[4 * k : 4 * k + 4]
+        for s, part in enumerate(parts):
+            out[64 * s : 64 * s + 64, :] = part[0:64, :]
+            out[256 + 64 * s : 320 + 64 * s, :] = part[64:128, :]
+        out[512:528, :] = merge_bias([p[128:144, :] for p in parts], 64)
+
+
+def arrange(body, parts, rows):
+    shape = jax.ShapeDtypeStruct((rows, parts[0].shape[1]), jnp.bfloat16)
+    return pl.pallas_call(
+        body,
+        in_specs=[pl.BlockSpec(memory_space=pltpu.VMEM)] * len(parts),
+        out_specs=[pl.BlockSpec(memory_space=pltpu.VMEM)] * 2,
+        out_shape=[shape, shape],
+        compiler_params=pltpu.CompilerParams(vmem_limit_bytes=16 * 2**20),
+    )(*parts)
+
+
 def ffn_tiles(x, weights):
-    total = None
-    lane = lax.broadcasted_iota(jnp.int32, (1, 256), 1) // 64
-    for first, second in zip(weights[::2], weights[1::2]):
-        up = jnp.concatenate([first[0:128, :], second[0:128, :]], axis=0)
-        down = jnp.concatenate([first[128:256, :], second[128:256, :]], axis=0)
-        b0 = first[256:272, 0:256].astype(jnp.float32)
-        b1 = second[256:272, 0:256].astype(jnp.float32)
-        bias = jnp.where(
-            lane < 2,
-            jnp.where(lane == 0, b0[0:1], b0[8:9]),
-            jnp.where(lane == 2, b1[0:1], b1[8:9]),
-        )
-        preact = lax.dot_general(x, up, nt, preferred_element_type=jnp.float32) + bias
-        active = gelu_exact(preact).astype(jnp.bfloat16)
-        part = jnp.dot(active, down, preferred_element_type=jnp.float32)
-        total = part if total is None else total + part
-    return total
+    up = jnp.concatenate([w[0:256, :] for w in weights], axis=0)
+    down = jnp.concatenate([w[256:512, :] for w in weights], axis=0)
+    bias = jnp.concatenate(
+        [w[512:528, 0:256].astype(jnp.float32)[0:1] for w in weights], axis=1
+    )
+    preact = lax.dot_general(x, up, nt, preferred_element_type=jnp.float32) + bias
+    active = gelu_exact(preact).astype(jnp.bfloat16)
+    return jnp.dot(active, down, preferred_element_type=jnp.float32)
 
 
 def ffn_kernel(count, first, last, meta, x_ref, *refs):
@@ -117,7 +146,7 @@
             out_ref[...] = total if first else acc_in[...] + total
 
         return
-    gain_ref, pooled_ref, sums = refs
+    gain_ref, graph_ref, pooled_ref, sums = refs
 
     @pl.when(i == 0)
     def _():
@@ -149,10 +178,11 @@
         tokens = jnp.ones((8, 1), jnp.float32)
         for s in range(6):
             tokens = jnp.where(seq == s, meta[6 + s].astype(jnp.float32), tokens)
-        pooled_ref[...] = (sums[...] / tokens).astype(jnp.bfloat16)
-
-
-def ffn_step(meta, packed, weights, acc=None, gain=None):
+        means = (sums[...] / tokens).astype(jnp.bfloat16)
+        pooled_ref[...] = jnp.where(seq < 6, means, graph_ref[...])
+
+
+def ffn_step(meta, packed, weights, acc=None, gain=None, graph_rows=None):
     rows, width = packed.shape
     count, first, last = len(weights), acc is None, gain is not None
     steps = rows // block_rows
@@ -165,15 +195,15 @@
         operands.append(acc)
     scratch = []
     if last:
-        in_specs.append(whole((1, width)))
-        operands.append(gain)
+        in_specs += [whole((1, width)), whole((8, width))]
+        operands += [gain, graph_rows]
         out_shape = jax.ShapeDtypeStruct((8, width), jnp.bfloat16)
         out_specs = whole((8, width))
         scratch = [pltpu.VMEM((8, width), jnp.float32)]
     else:
         out_shape = jax.ShapeDtypeStruct((rows, width), jnp.float32)
         out_specs = row_block
-    hidden = 128 * count
+    hidden = 256 * count
     return pl.pallas_call(
         functools.partial(ffn_kernel, count, first, last),
         grid_spec=pltpu.PrefetchScalarGridSpec(
@@ -185,7 +215,7 @@
         ),
         out_shape=out_shape,
         compiler_params=pltpu.CompilerParams(
-            dimension_semantics=("arbitrary",), vmem_limit_bytes=40 * 2**20
+            dimension_semantics=("arbitrary",), vmem_limit_bytes=56 * 2**20
         ),
         cost_estimate=pl.CostEstimate(
             flops=3 * rows * hidden * width, bytes_accessed=10 * 2**20, transcendentals=0
@@ -193,27 +223,30 @@
     )(meta, *operands)
 
 
-def tail_kernel(
-    place,
-    pooled_ref,
-    proj_ref,
-    graph_ref,
-    own_ref,
-    slot_ref,
-    loss_ref,
-    grad_graph_ref,
-    grad_text_ref,
-    grad_proj_ref,
-):
-    texts = pooled_ref.shape[0]
-    graphs = graph_ref.shape[0]
+def tail_kernel(place, *refs):
+    pieces, refs = refs[:8], refs[8:]
+    proj_ref, own_ref, slot_ref, gid_ref = refs[:4]
+    loss_ref, grad_graph_ref, grad_text_ref, grad_proj_ref = refs[4:]
     flat, row_first = place[0], place[1]
-    pooled = pooled_ref[...]
+    pooled = jnp.concatenate([p[...] for p in pieces], axis=0)
+    texts = pooled.shape[0]
+    graphs = gid_ref.shape[0]
+    devices = texts // 8
     text_emb = jnp.dot(pooled, proj_ref[...], preferred_element_type=jnp.float32)
     text_norm = jnp.sqrt(jnp.sum(text_emb * text_emb, axis=-1, keepdims=True) + epsilon)
     text_unit = text_emb / text_norm
     text_send = text_unit.astype(jnp.bfloat16)
-    graph_send = graph_ref[...]
+    line = lax.broadcasted_iota(jnp.int32, (2 * devices, texts), 0)
+    wanted = jnp.where(line < devices, 8 * line + 6, 8 * (line - devices) + 7)
+    carried = wanted == lax.broadcasted_iota(jnp.int32, (2 * devices, texts), 1)
+    carriers = jnp.dot(
+        carried.astype(jnp.bfloat16), pooled, preferred_element_type=jnp.float32
+    ).astype(jnp.bfloat16)
+    graph_send = jnp.concatenate(
+        [carriers[0:devices, 256 * k : 256 * k + 256] for k in range(4)]
+        + [carriers[devices:, 256 * k : 256 * k + 256] for k in range(2)],
+        axis=0,
+    )
     slot = slot_ref[...]
     valid = slot >= 0
 
@@ -228,7 +261,7 @@
     logits, expo, row_total = scores(graph_send)
     col_total = jnp.where(valid, jnp.sum(expo, axis=0, keepdims=True), 1.0)
     col_scale = 0.5 / col_total
-    matched = lax.broadcasted_iota(jnp.int32, (graphs, texts), 0) == slot
+    matched = gid_ref[...] == slot
     diagonal = jnp.sum(jnp.where(matched, logits, 0.0), axis=1, keepdims=True)
     row_terms = jnp.sum(jnp.log(row_total) - 2.0 * diagonal, axis=0, keepdims=True)
     col_terms = jnp.sum(jnp.log(col_total), axis=1, keepdims=True)
@@ -275,59 +308,37 @@
     grad_proj_ref[...] = grad_proj[0:8]
 
 
-def tail(place, pooled_all, proj_weight, graph_all, graph_emb, slot):
+def tail(place, pieces, proj_weight, graph_emb, slot, gid):
     shapes = [(1, 1), graph_emb.shape, (8, 256), (8, 256)]
     return pl.pallas_call(
         tail_kernel,
         in_specs=[pl.BlockSpec(memory_space=pltpu.SMEM)]
-        + [pl.BlockSpec(memory_space=pltpu.VMEM)] * 5,
+        + [pl.BlockSpec(memory_space=pltpu.VMEM)] * 12,
         out_specs=[pl.BlockSpec(memory_space=pltpu.VMEM)] * 4,
         out_shape=[jax.ShapeDtypeStruct(s, jnp.float32) for s in shapes],
         compiler_params=pltpu.CompilerParams(vmem_limit_bytes=48 * 2**20),
-    )(place, pooled_all, proj_weight, graph_all, graph_emb, slot)
+    )(place, *pieces, proj_weight, graph_emb, slot, gid)
 
 
 def gather_weights(up_weight, up_bias, down_weight):
     width = up_weight.shape[1]
-    bias_rows = jnp.pad(up_bias.reshape(1, 32), ((0, 7), (0, width - 32)))
-    own = jnp.concatenate([up_weight, down_weight, bias_rows], axis=0)
-    line = from_line(own, "dz")
-
-    def half(k):
-        up = [v[16 * k : 16 * k + 16] for v in line]
-        down = [v[32 + 16 * k : 48 + 16 * k] for v in line]
-        bias = jnp.concatenate([v[64:65, 16 * k : 16 * k + 16] for v in line], axis=1)
-        bias = jnp.pad(jnp.tile(bias, (1, width // 64)), ((0, 7), (0, 0)))
-        return jnp.concatenate(up + down + [bias], axis=0)
-
-    def join(a, b):
-        return jnp.concatenate(
-            [a[0:64], b[0:64], a[64:128], b[64:128], a[128:136], b[128:136]], axis=0
-        )
-
-    halves = []
-    for k, (inner, outer) in enumerate((("dx", "dy"), ("dy", "dx"))):
-        ring = [half(k)]
+    bias = [jnp.tile(b.reshape(1, 16), (16, width // 16)) for b in (up_bias[:16], up_bias[16:])]
+    own = jnp.concatenate([up_weight, down_weight, *bias], axis=0)
+    halves = arrange(split_kernel, from_line(own, "dz"), 144)
+    pieces = []
+    for half, inner in zip(halves, ("dx", "dy")):
+        ring = [half]
         for _ in range(3):
             ring.append(send(ring[-1], by_core=True, **{inner: 1}))
-        blocks = []
-        for start in (join(ring[0], ring[1]), join(ring[2], ring[3])):
-            steps = [start]
-            for _ in range(3):
-                steps.append(send(steps[-1], by_core=True, **{outer: 1}))
-            blocks.append(steps)
-        halves.append(blocks)
-    order = [(0, 0), (0, 1), (1, 0), (0, 2), (1, 1), (0, 3), (1, 2), (1, 3)]
-    groups = []
-    for at in range(0, 8, 2):
-        mine, other = [], []
-        for block, step in order[at : at + 2]:
-            for k in range(2):
-                value = halves[k][block][step]
-                mine.append(value)
-                other.append(send(value, dc=1))
-        groups.append(mine + other)
-    return groups
+        pieces += ring
+    pair = arrange(join_kernel, pieces, 528)
+    pairs_in_order = [pair]
+    for _ in range(3):
+        pair = [
+            send(block, by_core=True, **{outer: 1}) for block, outer in zip(pair, ("dy", "dx"))
+        ]
+        pairs_in_order.append(pair)
+    return pairs_in_order
 
 
 def shards(
@@ -349,19 +360,25 @@
     ).astype(jnp.int32)
 
     packed = pack_tokens(meta, text_hidden)
-    groups = gather_weights(up_weight, up_bias, down_weight)
     graph_norm = jnp.sqrt(jnp.sum(graph_emb * graph_emb, axis=-1, keepdims=True) + epsilon)
     graph_send = (graph_emb / graph_norm).astype(jnp.bfloat16)
-    graph_all = lax.all_gather(graph_send, "row", axis=0, tiled=True)
-
-    acc = None
-    for at, group in enumerate(groups):
-        gain = ln_gain.reshape(1, -1) if at == len(groups) - 1 else None
-        acc = ffn_step(meta, packed, group, acc, gain)
-    pooled = acc
-    for axis in ("dz", "dy", "dx"):
+    share = lax.dynamic_slice(graph_send, (col_index * 6, 0), (6, 256))
+    share = jnp.pad(share, ((0, 2), (0, 0))).reshape(2, 1024)
+    graph_rows = jnp.pad(share, ((6, 0), (0, 0)))
+
+    mine = gather_weights(up_weight, up_bias, down_weight)
+    other = [[send(block, dc=1) for block in pair] for pair in mine]
+    step = functools.partial(ffn_step, meta, packed)
+    acc = step(mine[0])
+    acc = step(other[0] + mine[1], acc)
+    acc = step(other[1] + mine[2], acc)
+    acc = step(other[2], acc)
+    acc = step(mine[3], acc)
+    pooled = step(other[3], acc, ln_gain.reshape(1, -1), graph_rows)
+    for axis in ("dz", "dy"):
         pooled = jnp.concatenate(from_line(pooled, axis), axis=0)
-    pooled_all = jnp.concatenate([pooled, send(pooled, dc=1)], axis=0)
+    line = from_line(pooled, "dx")
+    pieces = line + [send(value, dc=1) for value in line]
 
     rel = jnp.array([0, -1, 1, 2], jnp.int32)
     ids = flat_index(
@@ -376,8 +393,9 @@
     hit = tower[None, :] == jnp.arange(pairs_all, dtype=jnp.int32)[:, None]
     slot = jnp.sum(jnp.where(hit, perm[:, None] + 1, 0), axis=0, keepdims=True) - 1
     place = jnp.stack([flat, row_index * graph_emb.shape[0]]).astype(jnp.int32)
+    gid = (ids.reshape(1, -1) * 6 + jnp.arange(6, dtype=jnp.int32)[:, None]).reshape(-1, 1)
     loss, grad_graph, grad_text, grad_proj = tail(
-        place, pooled_all, proj_weight, graph_all, graph_emb, slot.astype(jnp.int32)
+        place, pieces, proj_weight, graph_emb, slot.astype(jnp.int32), gid
     )
     return (loss[0, 0], grad_graph, grad_text[:6], grad_proj)
 

time: 395 us -> 205 us (0.52)
  the two profiles are of different devices: /device:TPU:0 before, /device:TPU:1 now
where the time goes in v2:
time: 205 us; the launch traced here: 201 us
  starting transfers between devices  76.6 us (37%)
  Pallas kernels  69.8 us (34%)
  waiting for transfers between devices  41.2 us (20%)
  local copies, waits for them, and re-layouts  8.71 us (4%)
  other arithmetic  3.48 us (2%)
    ppermute x36, starting transfers between devices, send(): return lax.ppermute(value, axes, pairs(**hop))  76.6 us
    pallas_call x6, Pallas kernels, ffn_step(): pl.pallas_call(functools.partial(ffn_kernel, count, first, last), grid_sp...  61.3 us
    ppermute x36, waiting for transfers between devices, send(): return lax.ppermute(value, axes, pairs(**hop))  41.2 us
    pallas_call x1, Pallas kernels, tail(): pl.pallas_call(tail_kernel, in_specs=[pl.BlockSpec(memory_space=pltpu.SME...  6.19 us
    unnamed x32, local copies, waits for them, and re-layouts  6.06 us
  transfers between devices with their start and end apart: 36, of which 14 were waited for; matrix products, arithmetic and copies ran while one was open for 2% of the time, Pallas kernels for 25%

profile of v2, /device:TPU:1, one launch (start us, length us, event | category | flops | bytes accessed | tf_op | source)
XLA Modules:
  0.0 201.4 jit_solution(1726515602415502860)
XLA Ops:
  8.5 3.3 %collective-permute-done.refs_1_ = bf16[96,1024]{1,0:T(8,128)(2,1)S(1)} collective-permute-done((bf16[96,1024]{1,0:T(8,128)(2,1)S(1)}, bf16[96,1024]{1,0:T(8,128)(2,1)S(1)}, u32[]{:S(2)}, u32[]{:S(2)}) %collective-permute-start) | collective-permute-done | bytes 196640 | tf_op jit(solution)/shard_map/ppermute | solution.py:45
  11.8 5.1 %collective-permute-done.2.refs_3_ = bf16[96,1024]{1,0:T(8,128)(2,1)S(1)} collective-permute-done((bf16[96,1024]{1,0:T(8,128)(2,1)S(1)}, bf16[96,1024]{1,0:T(8,128)(2,1)S(1)}, u32[]{:S(2)}, u32[]{:S(2)}) %collective-permute-start.2) | collective-permute-done | bytes 196640 | tf_op jit(solution)/shard_map/ppermute | solution.py:45
  23.2 3.4 %collective-permute-start.4 = (bf16[144,1024]{1,0:T(8,128)(2,1)S(1)}, bf16[144,1024]{1,0:T(8,128)(2,1)S(1)}, u32[]{:S(2)}, u32[]{:S(2)}) collective-permute-start(bf16[144,1024]{1,0:T(8,128)(2,1)S(1)} %collective-permute-done.3.refs_1_), channel_id=1, source_target_pairs={{0,16},{1,19},{32,48},{33,51},{64,80},{65,83},{96,112},{97,115},{4... | collective-permute-start | bytes 884744 | tf_op jit(solution)/shard_map/ppermute | solution.py:45
  30.3 3.1 %collective-permute-start.5 = (bf16[144,1024]{1,0:T(8,128)(2,1)S(1)}, bf16[144,1024]{1,0:T(8,128)(2,1)S(1)}, u32[]{:S(2)}, u32[]{:S(2)}) collective-permute-start(bf16[144,1024]{1,0:T(8,128)(2,1)S(1)} %collective-permute-done.4.refs_2_), channel_id=1, source_target_pairs={{0,16},{1,19},{32,48},{33,51},{64,80},{65,83},{96,112},{97,115},{4... | collective-permute-start | bytes 884744 | tf_op jit(solution)/shard_map/ppermute | solution.py:45
  41.3 3.4 %collective-permute-start.9 = (bf16[528,1024]{1,0:T(8,128)(2,1)}, bf16[528,1024]{1,0:T(8,128)(2,1)}, u32[]{:S(2)}, u32[]{:S(2)}) collective-permute-start(bf16[528,1024]{1,0:T(8,128)(2,1)} %get-tuple-element.14.refs_0_), channel_id=1, source_target_pairs={{0,4},{1,13},{32,36},{33,45},{64,68},{65,77},{96,100},{97,109},{4,... | collective-permute-start | bytes 3244040 | tf_op jit(solution)/shard_map/ppermute | solution.py:45
  44.9 12.2 %collective-permute-done.9.refs_2_ = bf16[528,1024]{1,0:T(8,128)(2,1)} collective-permute-done((bf16[528,1024]{1,0:T(8,128)(2,1)}, bf16[528,1024]{1,0:T(8,128)(2,1)}, u32[]{:S(2)}, u32[]{:S(2)}) %collective-permute-start.9) | collective-permute-done | bytes 1081376 | tf_op jit(solution)/shard_map/ppermute | solution.py:45
  57.1 3.4 %collective-permute-start.10 = (bf16[528,1024]{1,0:T(8,128)(2,1)}, bf16[528,1024]{1,0:T(8,128)(2,1)}, u32[]{:S(2)}, u32[]{:S(2)}) collective-permute-start(bf16[528,1024]{1,0:T(8,128)(2,1)} %collective-permute-done.9.refs_2_), channel_id=1, source_target_pairs={{0,4},{1,13},{32,36},{33,45},{64,68},{65,77},{96,100},{97,109},{4,... | collective-permute-start | bytes 3244040 | tf_op jit(solution)/shard_map/ppermute | solution.py:45
  60.8 3.0 %collective-permute-start.21 = (bf16[528,1024]{1,0:T(8,128)(2,1)}, bf16[528,1024]{1,0:T(8,128)(2,1)}, u32[]{:S(2)}, u32[]{:S(2)}) collective-permute-start(bf16[528,1024]{1,0:T(8,128)(2,1)} %get-tuple-element.14.refs_0_), channel_id=1, source_target_pairs={{0,1},{1,0},{32,33},{33,32},{64,65},{65,64},{96,97},{97,96},{4,5},... | collective-permute-start | bytes 3244040 | tf_op jit(solution)/shard_map/ppermute | solution.py:45
  64.5 8.4 %collective-permute-done.10.refs_2_ = bf16[528,1024]{1,0:T(8,128)(2,1)} collective-permute-done((bf16[528,1024]{1,0:T(8,128)(2,1)}, bf16[528,1024]{1,0:T(8,128)(2,1)}, u32[]{:S(2)}, u32[]{:S(2)}) %collective-permute-start.10) | collective-permute-done | bytes 1081376 | tf_op jit(solution)/shard_map/ppermute | solution.py:45
  72.9 3.4 %collective-permute-start.11 = (bf16[528,1024]{1,0:T(8,128)(2,1)}, bf16[528,1024]{1,0:T(8,128)(2,1)}, u32[]{:S(2)}, u32[]{:S(2)}) collective-permute-start(bf16[528,1024]{1,0:T(8,128)(2,1)} %collective-permute-done.10.refs_2_), channel_id=1, source_target_pairs={{0,4},{1,13},{32,36},{33,45},{64,68},{65,77},{96,100},{97,109},{4,... | collective-permute-start | bytes 3244040 | tf_op jit(solution)/shard_map/ppermute | solution.py:45
  78.8 4.0 %collective-permute-start.20 = (bf16[528,1024]{1,0:T(8,128)(2,1)}, bf16[528,1024]{1,0:T(8,128)(2,1)}, u32[]{:S(2)}, u32[]{:S(2)}) collective-permute-start(bf16[528,1024]{1,0:T(8,128)(2,1)} %collective-permute-done.13.refs_3_), channel_id=1, source_target_pairs={{0,1},{1,0},{32,33},{33,32},{64,65},{65,64},{96,97},{97,96},{4,5},... | collective-permute-start | bytes 3244040 | tf_op jit(solution)/shard_map/ppermute | solution.py:45
  86.6 8.2 %shard_map.132.refs_4_ = f32[1536,1024]{1,0:T(8,128)} custom-call(s32[16]{0:T(128)} %copy-done.4, bf16[1536,1024]{1,0:T(8,128)(2,1)} %copy-done, bf16[528,1024]{1,0:T(8,128)(2,1)} %get-tuple-element.14.refs_0_, bf16[528,1024]{1,0:T(8,128)(2,1)} %get-tuple-element.15.refs_1_), custom_call_target="tpu_custom_call" | custom-call | flops 2415919104 | bytes 10485760 | tf_op jit(solution)/shard_map/pallas_call | solution.py:207
  96.6 11.9 %shard_map.133.refs_4_ = f32[1536,1024]{1,0:T(8,128)} custom-call(s32[16]{0:T(128)} %copy-done.4, bf16[1536,1024]{1,0:T(8,128)(2,1)} %copy-done, bf16[528,1024]{1,0:T(8,128)(2,1)} %collective-permute-done.21.refs_0_, bf16[528,1024]{1,0:T(8,128)(2,1)} %collective-permute-done.22.refs_1_, bf16[528,1024]{1,0:T(8,128)(2,1)} %collective-permute-done.9.refs_2_, ...), custom_call_target="tpu_custom_call" | custom-call | flops 4831838208 | bytes 10485760 | tf_op jit(solution)/shard_map/pallas_call | solution.py:207
  108.5 11.9 %shard_map.134.refs_2_ = f32[1536,1024]{1,0:T(8,128)} custom-call(s32[16]{0:T(128)} %copy-done.4, bf16[1536,1024]{1,0:T(8,128)(2,1)} %copy-done, bf16[528,1024]{1,0:T(8,128)(2,1)} %collective-permute-done.19.refs_0_, bf16[528,1024]{1,0:T(8,128)(2,1)} %collective-permute-done.20.refs_1_, bf16[528,1024]{1,0:T(8,128)(2,1)} %collective-permute-done.10.refs_2_, ...), custom_call_target="tpu_custom_call" | custom-call | flops 4831838208 | bytes 10485760 | tf_op jit(solution)/shard_map/pallas_call | solution.py:207
  122.4 9.0 %shard_map.135.refs_2_ = f32[1536,1024]{1,0:T(8,128)} custom-call(s32[16]{0:T(128)} %copy-done.4, bf16[1536,1024]{1,0:T(8,128)(2,1)} %copy-done, bf16[528,1024]{1,0:T(8,128)(2,1)} %copy-done.7, bf16[528,1024]{1,0:T(8,128)(2,1)} %copy-done.8, f32[1536,1024]{1,0:T(8,128)} %shard_map.134.refs_2_), custom_call_target="tpu_custom_call" | custom-call | flops 2415919104 | bytes 10485760 | tf_op jit(solution)/shard_map/pallas_call | solution.py:207
  131.4 9.0 %shard_map.136.refs_2_ = f32[1536,1024]{1,0:T(8,128)} custom-call(s32[16]{0:T(128)} %copy-done.4, bf16[1536,1024]{1,0:T(8,128)(2,1)} %copy-done, bf16[528,1024]{1,0:T(8,128)(2,1)} %collective-permute-done.11.refs_0_, bf16[528,1024]{1,0:T(8,128)(2,1)} %collective-permute-done.15.refs_1_, f32[1536,1024]{1,0:T(8,128)} %shard_map.135.refs_2_), custom_call_target="tpu_custom_call" | custom-call | flops 2415919104 | bytes 10485760 | tf_op jit(solution)/shard_map/pallas_call | solution.py:207
  141.9 11.1 %shard_map.137 = bf16[8,1024]{1,0:T(8,128)(2,1)} custom-call(s32[16]{0:T(128)} %copy-done.4, bf16[1536,1024]{1,0:T(8,128)(2,1)} %copy-done, bf16[528,1024]{1,0:T(8,128)(2,1)} %copy-done.5, bf16[528,1024]{1,0:T(8,128)(2,1)} %copy-done.6, f32[1536,1024]{1,0:T(8,128)} %shard_map.136.refs_2_, f32[1,1024]{1,0:T(1,128)} %bitcast.21, bf16[8,1024]{1,0:T(8,128)(2,1)} %pad.9.refs_4_), custom_call_target="tpu_custom_call" | custom-call | flops 2415919104 | bytes 10485760 | tf_op jit(solution)/shard_map/pallas_call | solution.py:207
  157.0 3.0 %collective-permute-done.25 = bf16[8,1024]{1,0:T(8,128)(2,1)S(1)} collective-permute-done((bf16[8,1024]{1,0:T(8,128)(2,1)}, bf16[8,1024]{1,0:T(8,128)(2,1)S(1)}, u32[]{:S(2)}, u32[]{:S(2)}) %collective-permute-start.25) | collective-permute-done | bytes 16416 | tf_op jit(solution)/shard_map/ppermute | solution.py:45
  160.9 7.7 %collective-permute-start.27 = (bf16[32,1024]{1,0:T(8,128)(2,1)S(1)}, bf16[32,1024]{1,0:T(8,128)(2,1)S(1)}, u32[]{:S(2)}, u32[]{:S(2)}) collective-permute-start(bf16[32,1024]{1,0:T(8,128)(2,1)S(1)} %pad_maximum_fusion.1), channel_id=1, source_target_pairs={{0,12},{1,13},{32,44},{33,45},{64,76},{65,77},{96,108},{97,109},{4... | collective-permute-start | bytes 196616 | tf_op jit(solution)/shard_map/ppermute | solution.py:45
  168.6 3.9 %collective-permute-start.28 = (bf16[32,1024]{1,0:T(8,128)(2,1)S(1)}, bf16[32,1024]{1,0:T(8,128)(2,1)S(1)}, u32[]{:S(2)}, u32[]{:S(2)}) collective-permute-start(bf16[32,1024]{1,0:T(8,128)(2,1)S(1)} %pad_maximum_fusion.1), channel_id=1, source_target_pairs={{0,8},{1,9},{32,40},{33,41},{64,72},{65,73},{96,104},{97,105},{4,1... | collective-permute-start | bytes 196616 | tf_op jit(solution)/shard_map/ppermute | solution.py:45
  174.2 4.6 %collective-permute-start.30 = (bf16[128,1024]{1,0:T(8,128)(2,1)S(1)}, bf16[128,1024]{1,0:T(8,128)(2,1)S(1)}, u32[]{:S(2)}, u32[]{:S(2)}) collective-permute-start(bf16[128,1024]{1,0:T(8,128)(2,1)S(1)} %constant_dynamic-update-slice_fusion.refs_0_), channel_id=1, source_target_pairs={{0,18},{1,19},{32,50},{33,51},{64,82},{65,83},{96,114},{97,115},{4... | collective-permute-start | bytes 786440 | tf_op jit(solution)/shard_map/ppermute | solution.py:45
  180.8 4.1 %collective-permute-start.32 = (bf16[128,1024]{1,0:T(8,128)(2,1)S(1)}, bf16[128,1024]{1,0:T(8,128)(2,1)S(1)}, u32[]{:S(2)}, u32[]{:S(2)}) collective-permute-start(bf16[128,1024]{1,0:T(8,128)(2,1)S(1)} %constant_dynamic-update-slice_fusion.refs_0_), channel_id=1, source_target_pairs={{0,1},{1,0},{32,33},{33,32},{64,65},{65,64},{96,97},{97,96},{4,5},... | collective-permute-start | bytes 786440 | tf_op jit(solution)/shard_map/ppermute | solution.py:45
  184.9 8.3 %collective-permute-start.33 = (bf16[128,1024]{1,0:T(8,128)(2,1)S(1)}, bf16[128,1024]{1,0:T(8,128)(2,1)S(1)}, u32[]{:S(2)}, u32[]{:S(2)}) collective-permute-start(bf16[128,1024]{1,0:T(8,128)(2,1)S(1)} %collective-permute-done.29.refs_1_), channel_id=1, source_target_pairs={{0,1},{1,0},{32,33},{33,32},{64,65},{65,64},{96,97},{97,96},{4,5},... | collective-permute-start | bytes 786440 | tf_op jit(solution)/shard_map/ppermute | solution.py:45
  195.2 6.2 %shard_map.138 = (f32[1,1]{1,0:T(1,128)}, f32[24,256]{1,0:T(8,128)}, f32[8,256]{1,0:T(8,128)}, f32[8,256]{1,0:T(8,128)}) custom-call(s32[2]{0:T(128)S(1)} %pad_add_fusion.place, bf16[128,1024]{1,0:T(8,128)(2,1)S(1)} %constant_dynamic-update-slice_fusion.refs_0_, bf16[128,1024]{1,0:T(8,128)(2,1)S(1)} %collective-permute-done.29.refs_1_, ...), custom_call_target="tpu_custom_call" | custom-call | tf_op jit(solution)/shard_map/pallas_call | solution.py:313
  (127 shorter events, 47.9 us)
Async XLA Ops:
  2.5 9.3 %collective-permute-start = (bf16[96,1024]{1,0:T(8,128)(2,1)S(1)}, bf16[96,1024]{1,0:T(8,128)(2,1)S(1)}, u32[]{:S(2)}, u32[]{:S(2)}) collective-permute-start(bf16[96,1024]{1,0:T(8,128)(2,1)S(1)} %pad_maximum_fusion.refs_0_), channel_id=1, source_target_pairs={{0,32},{1,33},{32,64},{33,65},{64,96},{65,97},{96,0},{97,1},{4,36}... | collective-permute-start | bytes 589832 | tf_op jit(solution)/shard_map/ppermute | solution.py:45
  7.3 9.6 %collective-permute-start.2 = (bf16[96,1024]{1,0:T(8,128)(2,1)S(1)}, bf16[96,1024]{1,0:T(8,128)(2,1)S(1)}, u32[]{:S(2)}, u32[]{:S(2)}) collective-permute-start(bf16[96,1024]{1,0:T(8,128)(2,1)S(1)} %pad_maximum_fusion.refs_0_), channel_id=1, source_target_pairs={{0,64},{1,65},{32,96},{33,97},{64,0},{65,1},{96,32},{97,33},{4,68}... | collective-permute-start | bytes 589832 | tf_op jit(solution)/shard_map/ppermute | solution.py:45
  23.2 7.1 %collective-permute-start.4 = (bf16[144,1024]{1,0:T(8,128)(2,1)S(1)}, bf16[144,1024]{1,0:T(8,128)(2,1)S(1)}, u32[]{:S(2)}, u32[]{:S(2)}) collective-permute-start(bf16[144,1024]{1,0:T(8,128)(2,1)S(1)} %collective-permute-done.3.refs_1_), channel_id=1, source_target_pairs={{0,16},{1,19},{32,48},{33,51},{64,80},{65,83},{96,112},{97,115},{4... | collective-permute-start | bytes 884744 | tf_op jit(solution)/shard_map/ppermute | solution.py:45
  41.3 15.8 %collective-permute-start.9 = (bf16[528,1024]{1,0:T(8,128)(2,1)}, bf16[528,1024]{1,0:T(8,128)(2,1)}, u32[]{:S(2)}, u32[]{:S(2)}) collective-permute-start(bf16[528,1024]{1,0:T(8,128)(2,1)} %get-tuple-element.14.refs_0_), channel_id=1, source_target_pairs={{0,4},{1,13},{32,36},{33,45},{64,68},{65,77},{96,100},{97,109},{4,... | collective-permute-start | bytes 3244040 | tf_op jit(solution)/shard_map/ppermute | solution.py:45
  44.7 15.8 %collective-permute-start.13 = (bf16[528,1024]{1,0:T(8,128)(2,1)}, bf16[528,1024]{1,0:T(8,128)(2,1)}, u32[]{:S(2)}, u32[]{:S(2)}) collective-permute-start(bf16[528,1024]{1,0:T(8,128)(2,1)} %get-tuple-element.15.refs_1_), channel_id=1, source_target_pairs={{0,16},{1,19},{32,48},{33,51},{64,80},{65,83},{96,112},{97,115},{4... | collective-permute-start | bytes 3244040 | tf_op jit(solution)/shard_map/ppermute | solution.py:45
  57.1 15.8 %collective-permute-start.10 = (bf16[528,1024]{1,0:T(8,128)(2,1)}, bf16[528,1024]{1,0:T(8,128)(2,1)}, u32[]{:S(2)}, u32[]{:S(2)}) collective-permute-start(bf16[528,1024]{1,0:T(8,128)(2,1)} %collective-permute-done.9.refs_2_), channel_id=1, source_target_pairs={{0,4},{1,13},{32,36},{33,45},{64,68},{65,77},{96,100},{97,109},{4,... | collective-permute-start | bytes 3244040 | tf_op jit(solution)/shard_map/ppermute | solution.py:45
  60.5 15.8 %collective-permute-start.14 = (bf16[528,1024]{1,0:T(8,128)(2,1)}, bf16[528,1024]{1,0:T(8,128)(2,1)}, u32[]{:S(2)}, u32[]{:S(2)}) collective-permute-start(bf16[528,1024]{1,0:T(8,128)(2,1)} %collective-permute-done.13.refs_3_), channel_id=1, source_target_pairs={{0,16},{1,19},{32,48},{33,51},{64,80},{65,83},{96,112},{97,115},{4... | collective-permute-start | bytes 3244040 | tf_op jit(solution)/shard_map/ppermute | solution.py:45
  60.8 18.0 %collective-permute-start.21 = (bf16[528,1024]{1,0:T(8,128)(2,1)}, bf16[528,1024]{1,0:T(8,128)(2,1)}, u32[]{:S(2)}, u32[]{:S(2)}) collective-permute-start(bf16[528,1024]{1,0:T(8,128)(2,1)} %get-tuple-element.14.refs_0_), channel_id=1, source_target_pairs={{0,1},{1,0},{32,33},{33,32},{64,65},{65,64},{96,97},{97,96},{4,5},... | collective-permute-start | bytes 3244040 | tf_op jit(solution)/shard_map/ppermute | solution.py:45
  63.9 22.1 %collective-permute-start.22 = (bf16[528,1024]{1,0:T(8,128)(2,1)}, bf16[528,1024]{1,0:T(8,128)(2,1)}, u32[]{:S(2)}, u32[]{:S(2)}) collective-permute-start(bf16[528,1024]{1,0:T(8,128)(2,1)} %get-tuple-element.15.refs_1_), channel_id=1, source_target_pairs={{0,1},{1,0},{32,33},{33,32},{64,65},{65,64},{96,97},{97,96},{4,5},... | collective-permute-start | bytes 3244040 | tf_op jit(solution)/shard_map/ppermute | solution.py:45
  63.9 22.2 %collective-permute-start.19 = (bf16[528,1024]{1,0:T(8,128)(2,1)}, bf16[528,1024]{1,0:T(8,128)(2,1)}, u32[]{:S(2)}, u32[]{:S(2)}) collective-permute-start(bf16[528,1024]{1,0:T(8,128)(2,1)} %collective-permute-done.9.refs_2_), channel_id=1, source_target_pairs={{0,1},{1,0},{32,33},{33,32},{64,65},{65,64},{96,97},{97,96},{4,5},... | collective-permute-start | bytes 3244040 | tf_op jit(solution)/shard_map/ppermute | solution.py:45
  72.9 21.9 %collective-permute-start.11 = (bf16[528,1024]{1,0:T(8,128)(2,1)}, bf16[528,1024]{1,0:T(8,128)(2,1)}, u32[]{:S(2)}, u32[]{:S(2)}) collective-permute-start(bf16[528,1024]{1,0:T(8,128)(2,1)} %collective-permute-done.10.refs_2_), channel_id=1, source_target_pairs={{0,4},{1,13},{32,36},{33,45},{64,68},{65,77},{96,100},{97,109},{4,... | collective-permute-start | bytes 3244040 | tf_op jit(solution)/shard_map/ppermute | solution.py:45
  76.3 19.9 %collective-permute-start.15 = (bf16[528,1024]{1,0:T(8,128)(2,1)}, bf16[528,1024]{1,0:T(8,128)(2,1)}, u32[]{:S(2)}, u32[]{:S(2)}) collective-permute-start(bf16[528,1024]{1,0:T(8,128)(2,1)} %collective-permute-done.14.refs_3_), channel_id=1, source_target_pairs={{0,16},{1,19},{32,48},{33,51},{64,80},{65,83},{96,112},{97,115},{4... | collective-permute-start | bytes 3244040 | tf_op jit(solution)/shard_map/ppermute | solution.py:45
  78.8 29.7 %collective-permute-start.20 = (bf16[528,1024]{1,0:T(8,128)(2,1)}, bf16[528,1024]{1,0:T(8,128)(2,1)}, u32[]{:S(2)}, u32[]{:S(2)}) collective-permute-start(bf16[528,1024]{1,0:T(8,128)(2,1)} %collective-permute-done.13.refs_3_), channel_id=1, source_target_pairs={{0,1},{1,0},{32,33},{33,32},{64,65},{65,64},{96,97},{97,96},{4,5},... | collective-permute-start | bytes 3244040 | tf_op jit(solution)/shard_map/ppermute | solution.py:45
  86.0 34.4 %collective-permute-start.17 = (bf16[528,1024]{1,0:T(8,128)(2,1)}, bf16[528,1024]{1,0:T(8,128)(2,1)S(1)}, u32[]{:S(2)}, u32[]{:S(2)}) collective-permute-start(bf16[528,1024]{1,0:T(8,128)(2,1)} %collective-permute-done.10.refs_2_), channel_id=1, source_target_pairs={{0,1},{1,0},{32,33},{33,32},{64,65},{65,64},{96,97},{97,96},{4,5},... | collective-permute-start | bytes 3244040 | tf_op jit(solution)/shard_map/ppermute | solution.py:45
  86.1 34.3 %collective-permute-start.18 = (bf16[528,1024]{1,0:T(8,128)(2,1)}, bf16[528,1024]{1,0:T(8,128)(2,1)S(1)}, u32[]{:S(2)}, u32[]{:S(2)}) collective-permute-start(bf16[528,1024]{1,0:T(8,128)(2,1)} %collective-permute-done.14.refs_3_), channel_id=1, source_target_pairs={{0,1},{1,0},{32,33},{33,32},{64,65},{65,64},{96,97},{97,96},{4,5},... | collective-permute-start | bytes 3244040 | tf_op jit(solution)/shard_map/ppermute | solution.py:45
  94.8 45.6 %collective-permute-start.12 = (bf16[528,1024]{1,0:T(8,128)(2,1)}, bf16[528,1024]{1,0:T(8,128)(2,1)S(1)}, u32[]{:S(2)}, u32[]{:S(2)}) collective-permute-start(bf16[528,1024]{1,0:T(8,128)(2,1)} %collective-permute-done.11.refs_0_), channel_id=1, source_target_pairs={{0,1},{1,0},{32,33},{33,32},{64,65},{65,64},{96,97},{97,96},{4,5},... | collective-permute-start | bytes 3244040 | tf_op jit(solution)/shard_map/ppermute | solution.py:45
  96.3 44.2 %collective-permute-start.16 = (bf16[528,1024]{1,0:T(8,128)(2,1)}, bf16[528,1024]{1,0:T(8,128)(2,1)S(1)}, u32[]{:S(2)}, u32[]{:S(2)}) collective-permute-start(bf16[528,1024]{1,0:T(8,128)(2,1)} %collective-permute-done.15.refs_1_), channel_id=1, source_target_pairs={{0,1},{1,0},{32,33},{33,32},{64,65},{65,64},{96,97},{97,96},{4,5},... | collective-permute-start | bytes 3244040 | tf_op jit(solution)/shard_map/ppermute | solution.py:45
  160.7 11.8 %collective-permute-start.26 = (bf16[32,1024]{1,0:T(8,128)(2,1)S(1)}, bf16[32,1024]{1,0:T(8,128)(2,1)S(1)}, u32[]{:S(2)}, u32[]{:S(2)}) collective-permute-start(bf16[32,1024]{1,0:T(8,128)(2,1)S(1)} %pad_maximum_fusion.1), channel_id=1, source_target_pairs={{0,4},{1,5},{32,36},{33,37},{64,68},{65,69},{96,100},{97,101},{4,8... | collective-permute-start | bytes 196616 | tf_op jit(solution)/shard_map/ppermute | solution.py:45
  160.9 11.6 %collective-permute-start.27 = (bf16[32,1024]{1,0:T(8,128)(2,1)S(1)}, bf16[32,1024]{1,0:T(8,128)(2,1)S(1)}, u32[]{:S(2)}, u32[]{:S(2)}) collective-permute-start(bf16[32,1024]{1,0:T(8,128)(2,1)S(1)} %pad_maximum_fusion.1), channel_id=1, source_target_pairs={{0,12},{1,13},{32,44},{33,45},{64,76},{65,77},{96,108},{97,109},{4... | collective-permute-start | bytes 196616 | tf_op jit(solution)/shard_map/ppermute | solution.py:45
  174.2 10.8 %collective-permute-start.29 = (bf16[128,1024]{1,0:T(8,128)(2,1)S(1)}, bf16[128,1024]{1,0:T(8,128)(2,1)S(1)}, u32[]{:S(2)}, u32[]{:S(2)}) collective-permute-start(bf16[128,1024]{1,0:T(8,128)(2,1)S(1)} %constant_dynamic-update-slice_fusion.refs_0_), channel_id=1, source_target_pairs={{0,16},{1,17},{32,48},{33,49},{64,80},{65,81},{96,112},{97,113},{4... | collective-permute-start | bytes 786440 | tf_op jit(solution)/shard_map/ppermute | solution.py:45
  174.2 19.1 %collective-permute-start.30 = (bf16[128,1024]{1,0:T(8,128)(2,1)S(1)}, bf16[128,1024]{1,0:T(8,128)(2,1)S(1)}, u32[]{:S(2)}, u32[]{:S(2)}) collective-permute-start(bf16[128,1024]{1,0:T(8,128)(2,1)S(1)} %constant_dynamic-update-slice_fusion.refs_0_), channel_id=1, source_target_pairs={{0,18},{1,19},{32,50},{33,51},{64,82},{65,83},{96,114},{97,115},{4... | collective-permute-start | bytes 786440 | tf_op jit(solution)/shard_map/ppermute | solution.py:45
  178.8 14.5 %collective-permute-start.31 = (bf16[128,1024]{1,0:T(8,128)(2,1)S(1)}, bf16[128,1024]{1,0:T(8,128)(2,1)S(1)}, u32[]{:S(2)}, u32[]{:S(2)}) collective-permute-start(bf16[128,1024]{1,0:T(8,128)(2,1)S(1)} %constant_dynamic-update-slice_fusion.refs_0_), channel_id=1, source_target_pairs={{0,2},{1,3},{32,34},{33,35},{64,66},{65,67},{96,98},{97,99},{4,6},... | collective-permute-start | bytes 786440 | tf_op jit(solution)/shard_map/ppermute | solution.py:45
  180.8 13.3 %collective-permute-start.32 = (bf16[128,1024]{1,0:T(8,128)(2,1)S(1)}, bf16[128,1024]{1,0:T(8,128)(2,1)S(1)}, u32[]{:S(2)}, u32[]{:S(2)}) collective-permute-start(bf16[128,1024]{1,0:T(8,128)(2,1)S(1)} %constant_dynamic-update-slice_fusion.refs_0_), channel_id=1, source_target_pairs={{0,1},{1,0},{32,33},{33,32},{64,65},{65,64},{96,97},{97,96},{4,5},... | collective-permute-start | bytes 786440 | tf_op jit(solution)/shard_map/ppermute | solution.py:45
  184.9 9.5 %collective-permute-start.33 = (bf16[128,1024]{1,0:T(8,128)(2,1)S(1)}, bf16[128,1024]{1,0:T(8,128)(2,1)S(1)}, u32[]{:S(2)}, u32[]{:S(2)}) collective-permute-start(bf16[128,1024]{1,0:T(8,128)(2,1)S(1)} %collective-permute-done.29.refs_1_), channel_id=1, source_target_pairs={{0,1},{1,0},{32,33},{33,32},{64,65},{65,64},{96,97},{97,96},{4,5},... | collective-permute-start | bytes 786440 | tf_op jit(solution)/shard_map/ppermute | solution.py:45
  (24 other events, 286.8 us)
